TPU v7x, 32 devices: a whole 2x2x4 slice. The times are simulated.
32 devices in a mesh: group: 2 (over x), cell: 16 (over z, y, core).
Axes of the slice: x: 2, y: 2, z: 4, core: 2. Of those that a mesh axis runs over, the one named last changes fastest.
Arguments:
- adjoint_seed: float32 [32, 5, 16384], P('group', None, 'cell'), parts along dimension 0, may hold values from -6 to 6
- inv_blocks: bfloat16 [32, 5, 5, 16384], P('group', None, None, 'cell'), parts along dimension 0
- flux_jacobians: float32 [2, 32, 5, 5], P(None, 'group'), parts along dimension 1, may hold values from -1.5 to 1.5
- modal_shapes: float32 [20, 5, 16384], P(None, None, 'cell'), may hold values from -0.01953125 to 0.01953125
- modal_gain: float32 [40], P('group'), parts along dimension 0, may hold values from 0.05 to 0.3
- face_cells: int32 [2, 49152], P(None, 'cell'), may hold values from 0 to 1279, as said below
- face_weights: float32 [49152], P('cell'), may hold values from 0.4 to 1
- colours: int32 [16384], P('cell'), may hold values from 0 to 1
- send_cells: int32 [2, 2048], P(None, 'cell'), may hold values from 0 to 1023, as said below
Outputs:
- adjoint_state: float32 [32, 5, 16384], P('group', None, 'cell'), parts along dimension 0
- modal_partials: float32 [32, 20], P('group'), parts along dimension 0
There are 2 independent parts, one for each index of `group`. A program takes and returns all parts, laid end to end along the dimension named above; an argument that names none is the same for every part. Nothing has to cross between parts.
Inputs may be any that keep to these rules, and one draw needn't show every extreme that they name: `face_cells`: each face's left cell is a local cell or a lower ghost (from 1024 to 1151); its right cell is a local cell or an upper ghost (from 1152 on). `send_cells`: within a partition the 256 listed cells are distinct local cells.
All inputs are finite; a program needn't handle non-finite values.
Results may differ from a plain program's by a relative error of at most 0.0003.
Values sent between devices are 32-bit elements; how exact they have to be, the bound alone decides.
A program may use at most 64 MiB of HBM per device.

v0:
```python
import functools
import math

import jax
import jax.numpy as jnp
from jax import lax
from jax.experimental import pallas as pl
from jax.experimental.pallas import tpu as pltpu
from jax.sharding import PartitionSpec as P

ITERS = 4
FREQUENCY = 0.04
F32 = jnp.float32
BF16 = jnp.bfloat16
F8 = jnp.float8_e4m3fn
LIFT = 256.0
MODE_ROWS = 32


def spectral_matrix(count):
    index = jnp.arange(count)
    apart = index[:, None] - index[None, :]
    angle = math.pi * apart.astype(F32) / count
    parity = jnp.where(apart % 2 == 0, 1.0, -1.0).astype(F32)
    safe_sin = jnp.where(apart == 0, 1.0, jnp.sin(angle))
    return jnp.where(apart == 0, 0.0, 0.5 * parity * jnp.cos(angle) / safe_sin)


def split(value):
    high = value.astype(BF16)
    return high, (value - high.astype(F32)).astype(BF16)


def mm(left, right):
    return jnp.dot(left, right, preferred_element_type=F32)


def mm_nt(left, right):
    return lax.dot_general(left, right, (((1,), (1,)), ((), ())), preferred_element_type=F32)


def kernel(
    n,
    seed_ref,
    inv_ref,
    w_in_ref,
    shapes_ref,
    gain_ref,
    faces_ref,
    g_ref,
    col_ref,
    send_ref,
    out_ref,
    part_ref,
    w_ref,
    gain_pad,
    left_hot,
    left_low,
    m_high,
    m_low,
    mg_high,
    mg_low,
    p_ref,
    sel_ref,
    x_ref,
    z_ref,
    base_ref,
    ab_ref,
    q_all,
    ghost_out,
    ghost_in,
    q_send,
    q_recv,
    g_send,
    g_recv,
):
    nvar, count, owned = seed_ref.shape
    modes = shapes_ref.shape[1]
    rows = count * nvar
    halo = send_ref.shape[1]
    nfaces = g_ref.shape[1]
    me = lax.axis_index("cell")
    peers = [lax.rem(me + d, n) for d in range(n)]

    barrier = pltpu.get_barrier_semaphore()
    for d in range(1, n):
        pl.semaphore_signal(barrier, inc=1, device_id={"cell": peers[d]}, device_id_type=pl.DeviceIdType.MESH)

    left = faces_ref[0:1, :]
    right = faces_ref[1:2, :]
    g_high, g_low = split(g_ref[...])
    one = jnp.ones((1, nfaces), BF16)
    step = 128
    tall = owned + halo

    def hot(index, start, size, value):
        lines = lax.broadcasted_iota(jnp.int32, (size, 128), 0).astype(jnp.int16)
        lines = jnp.concatenate([lines] * (nfaces // 128), axis=1)
        near = jnp.broadcast_to((index - start).astype(jnp.int16), (size, nfaces))
        zero = jnp.zeros((size, nfaces), BF16)
        return jnp.where(near == lines, jnp.broadcast_to(value, (size, nfaces)), zero)

    @pl.loop(0, tall // step)
    def _(t):
        at = pl.multiple_of(t * step, step)
        left_hot[pl.ds(at, step), :] = hot(left, at, step, g_high)
        left_low[pl.ds(at, step), :] = (hot(left, at, step, g_low).astype(F32) * LIFT).astype(F8)

    wide = 256
    tall_step = tall // 3

    @pl.loop(0, owned // wide)
    def _(t):
        at = pl.multiple_of(t * wide, wide)
        right_hot = hot(right, at, wide, one)
        right_low = right_hot.astype(F32).astype(F8)
        for part in range(3):
            r0 = part * tall_step
            block = mm_nt(left_hot[r0 : r0 + tall_step, :], right_hot)
            block = block + mm_nt(left_low[r0 : r0 + tall_step, :], right_low) * (1.0 / LIFT)
            high, low = split(block)
            here = min(r0 + tall_step, owned) - r0
            m_high[r0 : r0 + here, pl.ds(at, wide)] = high[:here]
            m_low[r0 : r0 + here, pl.ds(at, wide)] = low[:here]
            if here < tall_step:
                mg_high[0:halo, pl.ds(at, wide)] = high[here:]
                mg_low[0:halo, pl.ds(at, wide)] = low[here:]

    upper_high = hot(right, owned + halo, halo, g_high)
    upper_low = hot(right, owned + halo, halo, g_low)
    upper_hot = jnp.concatenate([upper_high, upper_low], axis=0)

    @pl.loop(0, owned // wide)
    def _(t):
        at = pl.multiple_of(t * wide, wide)
        block = mm_nt(upper_hot, hot(left, at, wide, one))
        high, low = split(block[:halo] + block[halo:])
        mg_high[halo:, pl.ds(at, wide)] = high
        mg_low[halo:, pl.ds(at, wide)] = low

    w_high, w_low = split(w_in_ref[...])
    lane = lax.broadcasted_iota(jnp.int32, (rows, 3 * rows), 1)
    line = lax.broadcasted_iota(jnp.int32, (rows, 3 * rows), 0)
    first = jnp.where((lane == line) | (lane == line + rows), 1.0, 0.0).astype(BF16)
    last = jnp.where(lane == line + 2 * rows, 1.0, 0.0).astype(BF16)
    w_ref[...] = (mm(w_high, first) + mm(w_low, last)).astype(BF16)
    gain_pad[...] = jnp.zeros((1, 128), F32)
    gain_pad[:, 0:modes] = gain_ref[...]
    send_row = jnp.concatenate([send_ref[0:1, :], send_ref[1:2, :]], axis=1)
    sel_ref[...] = jnp.where(
        send_row == lax.broadcasted_iota(jnp.int32, (owned, 2 * halo), 0), 1.0, 0.0
    ).astype(BF16)
    for v in range(nvar):
        shape_v = shapes_ref[v]
        shape_v = jnp.concatenate([shape_v, jnp.zeros((MODE_ROWS - modes, owned), F32)], axis=0)
        high, low = split(shape_v)
        p_ref[v, 0:MODE_ROWS, :] = high
        p_ref[v, MODE_ROWS:, :] = low
        z_ref[v * count : (v + 1) * count, :] = seed_ref[v]
    colours = col_ref[...]

    def update(colour):
        mask = colours == colour
        for w in range(nvar):
            spot = slice(w * count, (w + 1) * count)
            total = inv_ref[0, w].astype(F32) * z_ref[0:count, :]
            for v in range(1, nvar):
                total = total + inv_ref[v, w].astype(F32) * z_ref[v * count : (v + 1) * count, :]
            x_ref[spot, :] = jnp.where(mask, total, x_ref[spot, :])

    def coupling():
        high, low = split(x_ref[...])
        both = mm(w_ref[...], jnp.concatenate([high, low, high], axis=0))
        a_high, a_low = split(both[:rows])
        b_high, b_low = split(both[rows : 2 * rows])
        ab_ref[0, 0:rows, :] = a_high
        ab_ref[0, rows:, :] = a_low
        ab_ref[1, 0:rows, :] = b_high
        ab_ref[1, rows:, :] = b_low
        z_ref[...] = both[2 * rows :]

        @pl.loop(0, owned // wide)
        def _(t):
            at = pl.multiple_of(t * wide, wide)
            cols = pl.ds(at, wide)
            one = mm(ab_ref[0], m_high[:, cols]) + mm_nt(ab_ref[1], m_high[cols, :])
            two = mm(ab_ref[0, 0:rows, :], m_low[:, cols]) + mm_nt(ab_ref[1, 0:rows, :], m_low[cols, :])
            z_ref[:, cols] = z_ref[:, cols] + (one[:rows] + one[rows:] + two)

    def modal_copies(turn):
        return [
            pltpu.make_async_remote_copy(
                src_ref=q_all.at[turn, me],
                dst_ref=q_all.at[turn, me],
                send_sem=q_send.at[turn, d],
                recv_sem=q_recv.at[turn, d],
                device_id={"cell": peers[d]},
                device_id_type=pl.DeviceIdType.MESH,
            )
            for d in range(1, n)
        ]

    def ghost_copies(turn):
        return [
            pltpu.make_async_remote_copy(
                src_ref=ghost_out.at[turn, way],
                dst_ref=ghost_in.at[turn, 1 - way],
                send_sem=g_send.at[turn, way],
                recv_sem=g_recv.at[turn, way],
                device_id={"cell": peers[n - 1 if way == 0 else 1]},
                device_id_type=pl.DeviceIdType.MESH,
            )
            for way in range(2)
        ]

    def start_exchange(turn):
        high, low = split(x_ref[...])
        copies = []
        if turn < ITERS - 1:
            picked = mm(jnp.concatenate([high, low], axis=0), sel_ref[...])
            picked = picked[:rows] + picked[rows:]
            ghost_out[turn, 0] = picked[:, :halo]
            ghost_out[turn, 1] = picked[:, halo:]
            copies = ghost_copies(turn)
            if turn == 0:
                pl.semaphore_wait(barrier, n - 1)
            for copy in copies:
                copy.start()
        gram = jnp.zeros((2 * count, 2 * MODE_ROWS), F32)
        for v in range(nvar):
            spot = slice(v * count, (v + 1) * count)
            gram = gram + mm_nt(jnp.concatenate([high[spot], low[spot]], axis=0), p_ref[v])
        gram = gram[:count] + gram[count:]
        part = gram[:, :MODE_ROWS] + gram[:, MODE_ROWS:]
        half = count // 2
        q_all[turn, me] = jnp.concatenate(
            [part[:half], part[half:], jnp.zeros((half, 128 - 2 * MODE_ROWS), F32)], axis=1
        )
        modal = modal_copies(turn)
        for copy in modal:
            copy.start()
        return copies + modal

    def modal_sum(turn):
        total = q_all[turn, 0]
        for d in range(1, n):
            total = total + q_all[turn, d]
        return jnp.concatenate([total[:, :MODE_ROWS], total[:, MODE_ROWS : 2 * MODE_ROWS]], axis=0)

    x_ref[...] = jnp.zeros((rows, owned), F32)
    update(0)
    coupling()
    for v in range(nvar):
        spot = slice(v * count, (v + 1) * count)
        z_ref[spot, :] = seed_ref[v] - z_ref[spot, :]
    update(1)
    copies = start_exchange(0)
    for sweep in range(1, ITERS):
        coupling()
        for copy in copies:
            copy.wait()
        low_part = ghost_in[sweep - 1, 0]
        up_part = ghost_in[sweep - 1, 1]
        high, low = split(jnp.concatenate([low_part, up_part], axis=1))
        both = mm(w_ref[0 : 2 * rows, :], jnp.concatenate([high, low, high], axis=0))
        ghost_ab = jnp.concatenate([both[:rows, :halo], both[rows:, halo:]], axis=1)
        high, low = split(ghost_ab)
        term = mm(jnp.concatenate([high, low], axis=0), mg_high[...])
        term = term[:rows] + term[rows:] + mm(high, mg_low[...])
        lam = modal_sum(sweep - 1)[:, :MODE_ROWS] * gain_pad[:, :MODE_ROWS]
        lam_high, lam_low = split(lam)
        lam_both = jnp.concatenate([lam_high, lam_low], axis=0)
        for v in range(nvar):
            spot = slice(v * count, (v + 1) * count)
            lift = mm(lam_both, p_ref[v, 0:MODE_ROWS, :])
            lift = lift[:count] + lift[count:] + mm(lam_high, p_ref[v, MODE_ROWS:, :])
            base = seed_ref[v] + lift - term[spot]
            base_ref[spot, :] = base
            z_ref[spot, :] = base - z_ref[spot, :]
        update(0)
        coupling()
        z_ref[...] = base_ref[...] - z_ref[...]
        update(1)
        copies = start_exchange(sweep)
    for v in range(nvar):
        out_ref[v] = x_ref[v * count : (v + 1) * count, :]
    for copy in copies:
        copy.wait()
    part_ref[...] = modal_sum(ITERS - 1)[:, :modes]


def local(
    adjoint_seed,
    inv_blocks,
    flux_jacobians,
    modal_shapes,
    modal_gain,
    face_cells,
    face_weights,
    colours,
    send_cells,
):
    n = lax.axis_size("cell")
    count, nvar, owned = adjoint_seed.shape
    modes = modal_shapes.shape[0]
    rows = count * nvar
    halo = send_cells.shape[1]
    nfaces = face_weights.shape[0]
    eye_inst = jnp.eye(count, dtype=F32)
    eye_var = jnp.eye(nvar, dtype=F32)
    left_matrix = (
        jnp.transpose(flux_jacobians[0], (2, 0, 1))[:, :, :, None] * eye_inst[None, :, None, :]
    ).reshape(rows, rows)
    right_matrix = (
        jnp.transpose(flux_jacobians[1], (2, 0, 1))[:, :, :, None] * eye_inst[None, :, None, :]
    ).reshape(rows, rows)
    spectral = FREQUENCY * spectral_matrix(count)
    spectral_rows = (eye_var[:, None, :, None] * spectral.T[None, :, None, :]).reshape(rows, rows)
    stacked = jnp.concatenate([left_matrix, right_matrix, spectral_rows], axis=0)
    inverse = jnp.transpose(inv_blocks, (1, 2, 0, 3))
    vmem = pl.BlockSpec(memory_space=pltpu.VMEM)
    tall = owned + halo
    turns = ITERS
    out, part = pl.pallas_call(
        functools.partial(kernel, n),
        out_shape=(
            jax.ShapeDtypeStruct((nvar, count, owned), F32),
            jax.ShapeDtypeStruct((count, modes), F32),
        ),
        in_specs=[vmem] * 9,
        out_specs=(vmem, vmem),
        scratch_shapes=[
            pltpu.VMEM((3 * rows, 3 * rows), BF16),
            pltpu.VMEM((1, 128), F32),
            pltpu.VMEM((tall, nfaces), BF16),
            pltpu.VMEM((tall, nfaces), F8),
            pltpu.VMEM((owned, owned), BF16),
            pltpu.VMEM((owned, owned), BF16),
            pltpu.VMEM((2 * halo, owned), BF16),
            pltpu.VMEM((2 * halo, owned), BF16),
            pltpu.VMEM((nvar, 2 * MODE_ROWS, owned), BF16),
            pltpu.VMEM((owned, 2 * halo), BF16),
            pltpu.VMEM((rows, owned), F32),
            pltpu.VMEM((rows, owned), F32),
            pltpu.VMEM((rows, owned), F32),
            pltpu.VMEM((2, 2 * rows, owned), BF16),
            pltpu.VMEM((turns, n, count // 2, 128), F32),
            pltpu.VMEM((turns - 1, 2, rows, halo), F32),
            pltpu.VMEM((turns - 1, 2, rows, halo), F32),
            pltpu.SemaphoreType.DMA((turns, n)),
            pltpu.SemaphoreType.DMA((turns, n)),
            pltpu.SemaphoreType.DMA((turns - 1, 2)),
            pltpu.SemaphoreType.DMA((turns - 1, 2)),
        ],
        compiler_params=pltpu.CompilerParams(
            collective_id=0, has_side_effects=True, vmem_limit_bytes=56 * 1024 * 1024
        ),
    )(
        jnp.transpose(adjoint_seed, (1, 0, 2)),
        inverse,
        stacked,
        jnp.transpose(modal_shapes, (1, 0, 2)),
        modal_gain[None, :],
        face_cells,
        face_weights[None, :],
        colours[None, :],
        send_cells,
    )
    return jnp.transpose(out, (1, 0, 2)), part


def solution(mesh):
    return jax.shard_map(
        local,
        mesh=mesh,
        in_specs=(
            P("group", None, "cell"),
            P("group", None, None, "cell"),
            P(None, "group", None, None),
            P(None, None, "cell"),
            P("group"),
            P(None, "cell"),
            P("cell"),
            P("cell"),
            P(None, "cell"),
        ),
        out_specs=(P("group", None, "cell"), P("group", None)),
        check_vma=False,
    )
```

profile of v0, /device:TPU:0, one launch (start us, length us, event | category | flops | bytes accessed | tf_op | source)
XLA Modules:
  0.0 63.2 jit_solution(719075737222886705)
XLA Ops:
  0.6 0.8 %fusion.8 = (f32[1,16,5,5]{1,0,3,2:T(1,128)S(1)}, f32[1,16,5,5]{1,0,3,2:T(1,128)S(1)}) fusion(f32[2,16,5,5]{1,0,3,2:T(2,128)} %param.11), kind=kLoop, calls=%fused_computation.19 | loop fusion | bytes 6400 | tf_op jit(solution)/shard_map/slice | solution.py:312
  1.5 0.1 copy.19
  1.6 0.1 copy.20
  1.7 0.2 broadcast_multiply_fusion.2
  1.9 0.1 mul.86
  2.0 0.1 mul.89
  2.2 0.1 select_multiply_fusion
  2.2 0.1 broadcast_multiply_fusion
  2.3 0.1 mul.98
  2.5 0.7 %pad_maximum_fusion.w_in_ref = f32[240,80]{1,0:T(8,128)} fusion(f32[80,80]{1,0:T(8,128)S(1)} %mul.98, f32[80,80]{1,0:T(8,128)S(1)} %mul.89, f32[80,80]{1,0:T(8,128)S(1)} %mul.86), kind=kLoop, calls=%fused_computation.3 | loop fusion | flops 38400 | bytes 153600 | tf_op jit(solution)/shard_map/concatenate | solution.py:319
  3.1 57.7 %shard_map.104 = (f32[5,16,1024]{2,1,0:T(8,128)}, f32[16,20]{1,0:T(8,128)}) custom-call(f32[5,16,1024]{2,1,0:T(8,128)} %bitcast.18, bf16[5,5,16,1024]{3,2,1,0:T(8,128)(2,1)} %bitcast.15, f32[240,80]{1,0:T(8,128)} %pad_maximum_fusion.w_in_ref, f32[5,20,1024]{2,1,0:T(8,128)} %bitcast.16, f32[1,20]{1,0:T(1,128)} %bitcast.23, s32[2,3072]{1,0:T(2,128)} %faces_ref.1, ...), custom_call_target="tpu_custom_call" | custom-call | tf_op jit(solution)/shard_map/pallas_call | solution.py:324
  60.8 0.0 copy-start
  60.8 1.7 %copy.23 = f32[16,5,1024]{2,0,1:T(8,128)} copy(f32[16,5,1024]{2,0,1:T(8,128)} %bitcast.17) | data formatting | bytes 655360
  62.6 0.0 copy-done
  62.6 0.6 copy.24
  (2 shorter events, 0.0 us)
Async XLA Ops:
  60.8 1.7 %copy-start = (f32[16,20]{1,0:T(8,128)S(1)}, f32[16,20]{1,0:T(8,128)}, u32[]{:S(2)}) copy-start(f32[16,20]{1,0:T(8,128)} %get-tuple-element.13) | copy-start | bytes 3844
where the time goes:
time: 63.4 us; the launch traced here: 63.2 us
  Pallas kernels  57.7 us (91%)
  local copies, waits for them, and re-layouts  3.71 us (6%)
  other arithmetic  1.05 us (2%)
  between operations  0.7 us (1%)
    pallas_call x1, Pallas kernels, local(): pl.pallas_call(functools.partial(kernel, n), out_shape=(jax.ShapeDtypeStr...  57.7 us
    unnamed x4, local copies, waits for them, and re-layouts  2.33 us

commit v1 on v0

--- a/solution.py
+++ b/solution.py
@@ -12,18 +12,27 @@
 FREQUENCY = 0.04
 F32 = jnp.float32
 BF16 = jnp.bfloat16
-F8 = jnp.float8_e4m3fn
-LIFT = 256.0
 MODE_ROWS = 32
-
-
-def spectral_matrix(count):
-    index = jnp.arange(count)
-    apart = index[:, None] - index[None, :]
-    angle = math.pi * apart.astype(F32) / count
-    parity = jnp.where(apart % 2 == 0, 1.0, -1.0).astype(F32)
-    safe_sin = jnp.where(apart == 0, 1.0, jnp.sin(angle))
-    return jnp.where(apart == 0, 0.0, 0.5 * parity * jnp.cos(angle) / safe_sin)
+CANDIDATES = 64
+
+
+def spectral_weights(count):
+    return [FREQUENCY * 0.5 * (-1.0) ** d / math.tan(math.pi * d / count) for d in range(1, count)]
+
+
+def bf16_factors(value):
+    best_p = value.astype(BF16).astype(F32)
+    best_q = jnp.ones_like(value)
+    best = jnp.abs(value - best_p)
+    for k in range(1, CANDIDATES):
+        q = 1.0 + k / 128.0
+        p = (value * (1.0 / q)).astype(BF16).astype(F32)
+        miss = jnp.abs(value - p * q)
+        better = miss < best
+        best = jnp.where(better, miss, best)
+        best_p = jnp.where(better, p, best_p)
+        best_q = jnp.where(better, q, best_q)
+    return best_p.astype(BF16), best_q.astype(BF16)
 
 
 def split(value):
@@ -41,21 +50,25 @@
 
 def kernel(
     n,
-    seed_ref,
-    inv_ref,
-    w_in_ref,
-    shapes_ref,
+    seed_hbm,
+    inv_hbm,
+    flux_ref,
+    shapes_hbm,
     gain_ref,
     faces_ref,
     g_ref,
     col_ref,
     send_ref,
-    out_ref,
+    out_hbm,
     part_ref,
+    seed_ref,
+    inv_ref,
+    shapes_ref,
     w_ref,
     gain_pad,
     left_hot,
-    left_low,
+    right_hot,
+    upper_hot,
     m_high,
     m_low,
     mg_high,
@@ -69,6 +82,7 @@
     q_all,
     ghost_out,
     ghost_in,
+    in_sem,
     q_send,
     q_recv,
     g_send,
@@ -78,72 +92,93 @@
     modes = shapes_ref.shape[1]
     rows = count * nvar
     halo = send_ref.shape[1]
-    nfaces = g_ref.shape[1]
+    nfaces = faces_ref.shape[1]
     me = lax.axis_index("cell")
-    peers = [lax.rem(me + d, n) for d in range(n)]
+    lower, upper = lax.rem(me + n - 1, n), lax.rem(me + 1, n)
+    peers = partners(me, n)
+    loads = [
+        pltpu.make_async_copy(src, dst, in_sem.at[k])
+        for k, (src, dst) in enumerate(
+            [(seed_hbm, seed_ref), (shapes_hbm, shapes_ref), (inv_hbm, inv_ref)]
+        )
+    ]
+    for load in loads:
+        load.start()
 
     barrier = pltpu.get_barrier_semaphore()
     for d in range(1, n):
         pl.semaphore_signal(barrier, inc=1, device_id={"cell": peers[d]}, device_id_type=pl.DeviceIdType.MESH)
 
-    left = faces_ref[0:1, :]
-    right = faces_ref[1:2, :]
-    g_high, g_low = split(g_ref[...])
-    one = jnp.ones((1, nfaces), BF16)
+    left = faces_ref[0:1, :].astype(jnp.int16)
+    right = faces_ref[1:2, :].astype(jnp.int16)
+    p_tile, q_tile = bf16_factors(g_ref[...])
+    p_tile, q_tile = p_tile.astype(F32), q_tile.astype(F32)
+    p_row = jnp.concatenate([p_tile[k : k + 1, :] for k in range(nfaces // 128)], axis=1).astype(BF16)
+    q_row = jnp.concatenate([q_tile[k : k + 1, :] for k in range(nfaces // 128)], axis=1).astype(BF16)
     step = 128
     tall = owned + halo
 
     def hot(index, start, size, value):
         lines = lax.broadcasted_iota(jnp.int32, (size, 128), 0).astype(jnp.int16)
         lines = jnp.concatenate([lines] * (nfaces // 128), axis=1)
-        near = jnp.broadcast_to((index - start).astype(jnp.int16), (size, nfaces))
+        near = jnp.broadcast_to((index.astype(jnp.int32) - start).astype(jnp.int16), (size, nfaces))
         zero = jnp.zeros((size, nfaces), BF16)
         return jnp.where(near == lines, jnp.broadcast_to(value, (size, nfaces)), zero)
 
     @pl.loop(0, tall // step)
     def _(t):
         at = pl.multiple_of(t * step, step)
-        left_hot[pl.ds(at, step), :] = hot(left, at, step, g_high)
-        left_low[pl.ds(at, step), :] = (hot(left, at, step, g_low).astype(F32) * LIFT).astype(F8)
-
+        left_hot[pl.ds(at, step), :] = hot(left, at, step, p_row)
+
+    upper_hot[...] = hot(right, owned + halo, halo, q_row)
     wide = 256
-    tall_step = tall // 3
+    tall_step = owned // 2
 
     @pl.loop(0, owned // wide)
     def _(t):
         at = pl.multiple_of(t * wide, wide)
-        right_hot = hot(right, at, wide, one)
-        right_low = right_hot.astype(F32).astype(F8)
-        for part in range(3):
+        right_now = hot(right, at, wide, q_row)
+        right_hot[pl.ds(at, wide), :] = right_now
+        for part in range(owned // tall_step):
             r0 = part * tall_step
-            block = mm_nt(left_hot[r0 : r0 + tall_step, :], right_hot)
-            block = block + mm_nt(left_low[r0 : r0 + tall_step, :], right_low) * (1.0 / LIFT)
-            high, low = split(block)
-            here = min(r0 + tall_step, owned) - r0
-            m_high[r0 : r0 + here, pl.ds(at, wide)] = high[:here]
-            m_low[r0 : r0 + here, pl.ds(at, wide)] = low[:here]
-            if here < tall_step:
-                mg_high[0:halo, pl.ds(at, wide)] = high[here:]
-                mg_low[0:halo, pl.ds(at, wide)] = low[here:]
-
-    upper_high = hot(right, owned + halo, halo, g_high)
-    upper_low = hot(right, owned + halo, halo, g_low)
-    upper_hot = jnp.concatenate([upper_high, upper_low], axis=0)
-
-    @pl.loop(0, owned // wide)
-    def _(t):
-        at = pl.multiple_of(t * wide, wide)
-        block = mm_nt(upper_hot, hot(left, at, wide, one))
-        high, low = split(block[:halo] + block[halo:])
-        mg_high[halo:, pl.ds(at, wide)] = high
-        mg_low[halo:, pl.ds(at, wide)] = low
-
-    w_high, w_low = split(w_in_ref[...])
+            high, low = split(mm_nt(left_hot[r0 : r0 + tall_step, :], right_now))
+            m_high[r0 : r0 + tall_step, pl.ds(at, wide)] = high
+            m_low[r0 : r0 + tall_step, pl.ds(at, wide)] = low
+
+    def build_ghost_matrix():
+        @pl.loop(0, owned // wide)
+        def _(t):
+            at = pl.multiple_of(t * wide, wide)
+            high, low = split(mm_nt(left_hot[owned:tall, :], right_hot[pl.ds(at, wide), :]))
+            mg_high[0:halo, pl.ds(at, wide)] = high
+            mg_low[0:halo, pl.ds(at, wide)] = low
+            high, low = split(mm_nt(upper_hot[...], left_hot[pl.ds(at, wide), :]))
+            mg_high[halo:, pl.ds(at, wide)] = high
+            mg_low[halo:, pl.ds(at, wide)] = low
+
+    eye_line = lax.broadcasted_iota(jnp.int32, (count, rows), 0)
+    eye_lane = lax.broadcasted_iota(jnp.int32, (count, rows), 1)
+    eye = lax.rem(eye_lane, count) == eye_line
+    blocks = []
+    for side in range(2):
+        for w in range(nvar):
+            row = jnp.concatenate([flux_ref[v, w][side : side + 1, :] for v in range(nvar)], axis=1)
+            blocks.append(jnp.where(eye, jnp.broadcast_to(row, (count, rows)), 0.0))
+    line = lax.broadcasted_iota(jnp.int32, (rows, rows), 0)
+    lane = lax.broadcasted_iota(jnp.int32, (rows, rows), 1)
+    apart = lax.rem(lane, count) - lax.rem(line, count)
+    spectral = jnp.zeros((rows, rows), F32)
+    for d, weight in enumerate(spectral_weights(count), 1):
+        spectral = jnp.where(apart == d, weight, jnp.where(apart == -d, -weight, spectral))
+    spectral = jnp.where(lax.div(lane, count) == lax.div(line, count), spectral, 0.0)
+    w_high, w_low = split(jnp.concatenate(blocks + [spectral], axis=0))
     lane = lax.broadcasted_iota(jnp.int32, (rows, 3 * rows), 1)
     line = lax.broadcasted_iota(jnp.int32, (rows, 3 * rows), 0)
     first = jnp.where((lane == line) | (lane == line + rows), 1.0, 0.0).astype(BF16)
     last = jnp.where(lane == line + 2 * rows, 1.0, 0.0).astype(BF16)
     w_ref[...] = (mm(w_high, first) + mm(w_low, last)).astype(BF16)
+    for load in loads:
+        load.wait()
     gain_pad[...] = jnp.zeros((1, 128), F32)
     gain_pad[:, 0:modes] = gain_ref[...]
     send_row = jnp.concatenate([send_ref[0:1, :], send_ref[1:2, :]], axis=1)
@@ -197,7 +232,7 @@
                 device_id={"cell": peers[d]},
                 device_id_type=pl.DeviceIdType.MESH,
             )
-            for d in range(1, n)
+            for d in range(n - 1, 0, -1)
         ]
 
     def ghost_copies(turn):
@@ -207,7 +242,7 @@
                 dst_ref=ghost_in.at[turn, 1 - way],
                 send_sem=g_send.at[turn, way],
                 recv_sem=g_recv.at[turn, way],
-                device_id={"cell": peers[n - 1 if way == 0 else 1]},
+                device_id={"cell": lower if way == 0 else upper},
                 device_id_type=pl.DeviceIdType.MESH,
             )
             for way in range(2)
@@ -255,6 +290,7 @@
         z_ref[spot, :] = seed_ref[v] - z_ref[spot, :]
     update(1)
     copies = start_exchange(0)
+    build_ghost_matrix()
     for sweep in range(1, ITERS):
         coupling()
         for copy in copies:
@@ -282,11 +318,36 @@
         z_ref[...] = base_ref[...] - z_ref[...]
         update(1)
         copies = start_exchange(sweep)
-    for v in range(nvar):
-        out_ref[v] = x_ref[v * count : (v + 1) * count, :]
+    store = pltpu.make_async_copy(x_ref, out_hbm, in_sem.at[0])
+    store.start()
     for copy in copies:
         copy.wait()
     part_ref[...] = modal_sum(ITERS - 1)[:, :modes]
+    store.wait()
+
+
+def partners(me, n):
+    if n & (n - 1):
+        return [lax.rem(me + d, n) for d in range(n)]
+    places = []
+    for d in range(n):
+        place = me
+        bit = 1
+        while bit < n:
+            if d & bit:
+                place = place + bit - 2 * bit * lax.rem(lax.div(me, bit), 2)
+            bit *= 2
+        places.append(place)
+    return places
+
+
+def hand_over(out_ref, part_ref, out_final, part_final, sem):
+    first = pltpu.make_async_copy(out_ref, out_final, sem.at[0])
+    second = pltpu.make_async_copy(part_ref, part_final, sem.at[1])
+    first.start()
+    second.start()
+    first.wait()
+    second.wait()
 
 
 def local(
@@ -306,34 +367,28 @@
     rows = count * nvar
     halo = send_cells.shape[1]
     nfaces = face_weights.shape[0]
-    eye_inst = jnp.eye(count, dtype=F32)
-    eye_var = jnp.eye(nvar, dtype=F32)
-    left_matrix = (
-        jnp.transpose(flux_jacobians[0], (2, 0, 1))[:, :, :, None] * eye_inst[None, :, None, :]
-    ).reshape(rows, rows)
-    right_matrix = (
-        jnp.transpose(flux_jacobians[1], (2, 0, 1))[:, :, :, None] * eye_inst[None, :, None, :]
-    ).reshape(rows, rows)
-    spectral = FREQUENCY * spectral_matrix(count)
-    spectral_rows = (eye_var[:, None, :, None] * spectral.T[None, :, None, :]).reshape(rows, rows)
-    stacked = jnp.concatenate([left_matrix, right_matrix, spectral_rows], axis=0)
     inverse = jnp.transpose(inv_blocks, (1, 2, 0, 3))
     vmem = pl.BlockSpec(memory_space=pltpu.VMEM)
+    hbm = pl.BlockSpec(memory_space=pl.ANY)
     tall = owned + halo
     turns = ITERS
     out, part = pl.pallas_call(
         functools.partial(kernel, n),
         out_shape=(
-            jax.ShapeDtypeStruct((nvar, count, owned), F32),
+            jax.ShapeDtypeStruct((rows, owned), F32),
             jax.ShapeDtypeStruct((count, modes), F32),
         ),
-        in_specs=[vmem] * 9,
-        out_specs=(vmem, vmem),
+        in_specs=[hbm, hbm, vmem, hbm] + [vmem] * 5,
+        out_specs=(hbm, vmem),
         scratch_shapes=[
+            pltpu.VMEM((nvar, count, owned), F32),
+            pltpu.VMEM((nvar, nvar, count, owned), BF16),
+            pltpu.VMEM((nvar, modes, owned), F32),
             pltpu.VMEM((3 * rows, 3 * rows), BF16),
             pltpu.VMEM((1, 128), F32),
             pltpu.VMEM((tall, nfaces), BF16),
-            pltpu.VMEM((tall, nfaces), F8),
+            pltpu.VMEM((owned, nfaces), BF16),
+            pltpu.VMEM((halo, nfaces), BF16),
             pltpu.VMEM((owned, owned), BF16),
             pltpu.VMEM((owned, owned), BF16),
             pltpu.VMEM((2 * halo, owned), BF16),
@@ -347,6 +402,7 @@
             pltpu.VMEM((turns, n, count // 2, 128), F32),
             pltpu.VMEM((turns - 1, 2, rows, halo), F32),
             pltpu.VMEM((turns - 1, 2, rows, halo), F32),
+            pltpu.SemaphoreType.DMA((3,)),
             pltpu.SemaphoreType.DMA((turns, n)),
             pltpu.SemaphoreType.DMA((turns, n)),
             pltpu.SemaphoreType.DMA((turns - 1, 2)),
@@ -358,15 +414,25 @@
     )(
         jnp.transpose(adjoint_seed, (1, 0, 2)),
         inverse,
-        stacked,
+        jnp.transpose(flux_jacobians, (2, 3, 0, 1)),
         jnp.transpose(modal_shapes, (1, 0, 2)),
         modal_gain[None, :],
         face_cells,
-        face_weights[None, :],
+        face_weights.reshape(nfaces // 128, 128),
         colours[None, :],
         send_cells,
     )
-    return jnp.transpose(out, (1, 0, 2)), part
+    out, part = pl.pallas_call(
+        hand_over,
+        out_shape=(
+            jax.ShapeDtypeStruct((rows, owned), F32),
+            jax.ShapeDtypeStruct((count, modes), F32),
+        ),
+        in_specs=[hbm, hbm],
+        out_specs=(hbm, hbm),
+        scratch_shapes=[pltpu.SemaphoreType.DMA((2,))],
+    )(out, part)
+    return jnp.transpose(out.reshape(nvar, count, owned), (1, 0, 2)), part
 
 
 def solution(mesh):

time: 63.4 us -> 65.1 us (1.027)
  Pallas kernels: 57.7 us -> 64.2 us
  local copies, waits for them, and re-layouts: 3.71 us -> 0 us
  other arithmetic: 1.05 us -> 0 us
    pallas_call x0 -> x1, Pallas kernels: none -> 11.3 us  [local(): pl.pallas_call(hand_over, out_shape=(jax.ShapeDtypeStruct((rows, owned),...]
    pallas_call x1, Pallas kernels: 57.7 us -> 53 us  [local(): pl.pallas_call(functools.partial(kernel, n), out_shape=(jax.ShapeDtypeStr...]
    unnamed x4 -> x0, local copies, waits for them, and re-layouts: 2.33 us -> none
    slice x1 -> x0, local copies, waits for them, and re-layouts: 0.84 us -> none  [local(): flux_jacobians[0]]
    concatenate x1 -> x0, other arithmetic: 0.66 us -> none  [local(): jnp.concatenate([left_matrix, right_matrix, spectral_rows], axis=0)]
where the time goes in v1:
time: 65.1 us; the launch traced here: 64.9 us
  Pallas kernels  64.2 us (99%)
    pallas_call x1, Pallas kernels, local(): pl.pallas_call(functools.partial(kernel, n), out_shape=(jax.ShapeDtypeStr...  53 us
    pallas_call x1, Pallas kernels, local(): pl.pallas_call(hand_over, out_shape=(jax.ShapeDtypeStruct((rows, owned),...  11.3 us

profile of v1, /device:TPU:0, one launch (start us, length us, event | category | flops | bytes accessed | tf_op | source)
XLA Modules:
  0.0 64.9 jit_solution(11049678827712887107)
XLA Ops:
  0.6 53.0 %shard_map.104 = (f32[80,1024]{1,0:T(8,128)}, f32[16,20]{1,0:T(8,128)}) custom-call(f32[5,16,1024]{2,1,0:T(8,128)} %bitcast.12, bf16[5,5,16,1024]{3,2,1,0:T(8,128)(2,1)} %bitcast.10, f32[5,5,2,16]{3,2,1,0:T(2,128)} %bitcast.13, f32[5,20,1024]{2,1,0:T(8,128)} %bitcast.11, f32[1,20]{1,0:T(1,128)} %bitcast.16, s32[2,3072]{1,0:T(2,128)} %faces_ref.1, ...), custom_call_target="tpu_custom_call" | custom-call | tf_op jit(solution)/shard_map/pallas_call | solution.py:375
  53.6 11.3 %shard_map.105 = (f32[80,1024]{1,0:T(8,128)}, f32[16,20]{1,0:T(8,128)}) custom-call(f32[80,1024]{1,0:T(8,128)} %get-tuple-element.6.out_ref, f32[16,20]{1,0:T(8,128)} %get-tuple-element.7.part_ref), custom_call_target="tpu_custom_call" | custom-call | tf_op jit(solution)/shard_map/pallas_call | solution.py:425

commit v2 on v1

--- a/solution.py
+++ b/solution.py
@@ -132,6 +132,7 @@
 
     upper_hot[...] = hot(right, owned + halo, halo, q_row)
     wide = 256
+    broad = 1024
     tall_step = owned // 2
 
     @pl.loop(0, owned // wide)
@@ -214,10 +215,10 @@
         ab_ref[1, rows:, :] = b_low
         z_ref[...] = both[2 * rows :]
 
-        @pl.loop(0, owned // wide)
+        @pl.loop(0, owned // broad)
         def _(t):
-            at = pl.multiple_of(t * wide, wide)
-            cols = pl.ds(at, wide)
+            at = pl.multiple_of(t * broad, broad)
+            cols = pl.ds(at, broad)
             one = mm(ab_ref[0], m_high[:, cols]) + mm_nt(ab_ref[1], m_high[cols, :])
             two = mm(ab_ref[0, 0:rows, :], m_low[:, cols]) + mm_nt(ab_ref[1, 0:rows, :], m_low[cols, :])
             z_ref[:, cols] = z_ref[:, cols] + (one[:rows] + one[rows:] + two)
@@ -250,17 +251,21 @@
 
     def start_exchange(turn):
         high, low = split(x_ref[...])
-        copies = []
-        if turn < ITERS - 1:
+
+        @pl.when(turn < ITERS - 1)
+        def _():
             picked = mm(jnp.concatenate([high, low], axis=0), sel_ref[...])
             picked = picked[:rows] + picked[rows:]
             ghost_out[turn, 0] = picked[:, :halo]
             ghost_out[turn, 1] = picked[:, halo:]
-            copies = ghost_copies(turn)
-            if turn == 0:
+
+            @pl.when(turn == 0)
+            def _():
                 pl.semaphore_wait(barrier, n - 1)
-            for copy in copies:
+
+            for copy in ghost_copies(turn):
                 copy.start()
+
         gram = jnp.zeros((2 * count, 2 * MODE_ROWS), F32)
         for v in range(nvar):
             spot = slice(v * count, (v + 1) * count)
@@ -271,10 +276,8 @@
         q_all[turn, me] = jnp.concatenate(
             [part[:half], part[half:], jnp.zeros((half, 128 - 2 * MODE_ROWS), F32)], axis=1
         )
-        modal = modal_copies(turn)
-        for copy in modal:
+        for copy in modal_copies(turn):
             copy.start()
-        return copies + modal
 
     def modal_sum(turn):
         total = q_all[turn, 0]
@@ -283,44 +286,49 @@
         return jnp.concatenate([total[:, :MODE_ROWS], total[:, MODE_ROWS : 2 * MODE_ROWS]], axis=0)
 
     x_ref[...] = jnp.zeros((rows, owned), F32)
-    update(0)
-    coupling()
     for v in range(nvar):
-        spot = slice(v * count, (v + 1) * count)
-        z_ref[spot, :] = seed_ref[v] - z_ref[spot, :]
-    update(1)
-    copies = start_exchange(0)
-    build_ghost_matrix()
-    for sweep in range(1, ITERS):
-        coupling()
-        for copy in copies:
-            copy.wait()
-        low_part = ghost_in[sweep - 1, 0]
-        up_part = ghost_in[sweep - 1, 1]
-        high, low = split(jnp.concatenate([low_part, up_part], axis=1))
-        both = mm(w_ref[0 : 2 * rows, :], jnp.concatenate([high, low, high], axis=0))
-        ghost_ab = jnp.concatenate([both[:rows, :halo], both[rows:, halo:]], axis=1)
-        high, low = split(ghost_ab)
-        term = mm(jnp.concatenate([high, low], axis=0), mg_high[...])
-        term = term[:rows] + term[rows:] + mm(high, mg_low[...])
-        lam = modal_sum(sweep - 1)[:, :MODE_ROWS] * gain_pad[:, :MODE_ROWS]
-        lam_high, lam_low = split(lam)
-        lam_both = jnp.concatenate([lam_high, lam_low], axis=0)
-        for v in range(nvar):
-            spot = slice(v * count, (v + 1) * count)
-            lift = mm(lam_both, p_ref[v, 0:MODE_ROWS, :])
-            lift = lift[:count] + lift[count:] + mm(lam_high, p_ref[v, MODE_ROWS:, :])
-            base = seed_ref[v] + lift - term[spot]
-            base_ref[spot, :] = base
-            z_ref[spot, :] = base - z_ref[spot, :]
+        base_ref[v * count : (v + 1) * count, :] = seed_ref[v]
+
+    @pl.loop(0, ITERS)
+    def _(sweep):
+        @pl.when(sweep > 0)
+        def _():
+            coupling()
+
+            @pl.when(sweep == 1)
+            def _():
+                build_ghost_matrix()
+
+            for copy in ghost_copies(sweep - 1) + modal_copies(sweep - 1):
+                copy.wait()
+            low_part = ghost_in[sweep - 1, 0]
+            up_part = ghost_in[sweep - 1, 1]
+            high, low = split(jnp.concatenate([low_part, up_part], axis=1))
+            both = mm(w_ref[0 : 2 * rows, :], jnp.concatenate([high, low, high], axis=0))
+            ghost_ab = jnp.concatenate([both[:rows, :halo], both[rows:, halo:]], axis=1)
+            high, low = split(ghost_ab)
+            term = mm(jnp.concatenate([high, low], axis=0), mg_high[...])
+            term = term[:rows] + term[rows:] + mm(high, mg_low[...])
+            lam = modal_sum(sweep - 1)[:, :MODE_ROWS] * gain_pad[:, :MODE_ROWS]
+            lam_high, lam_low = split(lam)
+            lam_both = jnp.concatenate([lam_high, lam_low], axis=0)
+            for v in range(nvar):
+                spot = slice(v * count, (v + 1) * count)
+                lift = mm(lam_both, p_ref[v, 0:MODE_ROWS, :])
+                lift = lift[:count] + lift[count:] + mm(lam_high, p_ref[v, MODE_ROWS:, :])
+                base = seed_ref[v] + lift - term[spot]
+                base_ref[spot, :] = base
+                z_ref[spot, :] = base - z_ref[spot, :]
+
         update(0)
         coupling()
         z_ref[...] = base_ref[...] - z_ref[...]
         update(1)
-        copies = start_exchange(sweep)
+        start_exchange(sweep)
+
     store = pltpu.make_async_copy(x_ref, out_hbm, in_sem.at[0])
     store.start()
-    for copy in copies:
+    for copy in modal_copies(ITERS - 1):
         copy.wait()
     part_ref[...] = modal_sum(ITERS - 1)[:, :modes]
     store.wait()
@@ -341,13 +349,21 @@
     return places
 
 
-def hand_over(out_ref, part_ref, out_final, part_final, sem):
-    first = pltpu.make_async_copy(out_ref, out_final, sem.at[0])
-    second = pltpu.make_async_copy(part_ref, part_final, sem.at[1])
-    first.start()
-    second.start()
-    first.wait()
-    second.wait()
+def hand_over(out_ref, part_ref, out_final, part_final, stage, small, sem):
+    pieces = 5
+    size = out_ref.shape[0] // pieces
+    spots = [pl.ds(k * size, size) for k in range(pieces)]
+    ins = [pltpu.make_async_copy(out_ref.at[s], stage.at[s], sem.at[0, k]) for k, s in enumerate(spots)]
+    outs = [pltpu.make_async_copy(stage.at[s], out_final.at[s], sem.at[1, k]) for k, s in enumerate(spots)]
+    ins.append(pltpu.make_async_copy(part_ref, small, sem.at[0, pieces]))
+    outs.append(pltpu.make_async_copy(small, part_final, sem.at[1, pieces]))
+    for copy in ins:
+        copy.start()
+    for first, second in zip(ins, outs):
+        first.wait()
+        second.start()
+    for copy in outs:
+        copy.wait()
 
 
 def local(
@@ -430,7 +446,11 @@
         ),
         in_specs=[hbm, hbm],
         out_specs=(hbm, hbm),
-        scratch_shapes=[pltpu.SemaphoreType.DMA((2,))],
+        scratch_shapes=[
+            pltpu.VMEM((rows, owned), F32),
+            pltpu.VMEM((count, modes), F32),
+            pltpu.SemaphoreType.DMA((2, 6)),
+        ],
     )(out, part)
     return jnp.transpose(out.reshape(nvar, count, owned), (1, 0, 2)), part
 

time: 65.1 us -> 52.7 us (0.81)
  Pallas kernels: 64.2 us -> 51.8 us
    pallas_call x1, Pallas kernels: 11.3 us -> 1.7 us  [local(): pl.pallas_call(hand_over, out_shape=(jax.ShapeDtypeStruct((rows, owned),...]
    pallas_call x1, Pallas kernels: 53 us -> 50.1 us  [local(): pl.pallas_call(functools.partial(kernel, n), out_shape=(jax.ShapeDtypeStr...]
where the time goes in v2:
time: 52.7 us; the launch traced here: 52.4 us
  Pallas kernels  51.8 us (98%)
  between operations  0.64 us (1%)
    pallas_call x1, Pallas kernels, local(): pl.pallas_call(functools.partial(kernel, n), out_shape=(jax.ShapeDtypeStr...  50.1 us
    pallas_call x1, Pallas kernels, local(): pl.pallas_call(hand_over, out_shape=(jax.ShapeDtypeStruct((rows, owned),...  1.7 us

profile of v2, /device:TPU:0, one launch (start us, length us, event | category | flops | bytes accessed | tf_op | source)
XLA Modules:
  0.0 52.4 jit_solution(6544353752993890688)
XLA Ops:
  0.6 50.1 %shard_map.104 = (f32[80,1024]{1,0:T(8,128)}, f32[16,20]{1,0:T(8,128)}) custom-call(f32[5,16,1024]{2,1,0:T(8,128)} %bitcast.12, bf16[5,5,16,1024]{3,2,1,0:T(8,128)(2,1)} %bitcast.10, f32[5,5,2,16]{3,2,1,0:T(2,128)} %bitcast.13, f32[5,20,1024]{2,1,0:T(8,128)} %bitcast.11, f32[1,20]{1,0:T(1,128)} %bitcast.16, s32[2,3072]{1,0:T(2,128)} %faces_ref.1, ...), custom_call_target="tpu_custom_call" | custom-call | tf_op jit(solution)/shard_map/pallas_call | solution.py:391
  50.7 1.7 %shard_map.105 = (f32[80,1024]{1,0:T(8,128)}, f32[16,20]{1,0:T(8,128)}) custom-call(f32[80,1024]{1,0:T(8,128)} %get-tuple-element.6.out_ref, f32[16,20]{1,0:T(8,128)} %get-tuple-element.7.part_ref), custom_call_target="tpu_custom_call" | custom-call | tf_op jit(solution)/shard_map/pallas_call | solution.py:441

commit v3 on v2

--- a/solution.py
+++ b/solution.py
@@ -12,7 +12,11 @@
 FREQUENCY = 0.04
 F32 = jnp.float32
 BF16 = jnp.bfloat16
-MODE_ROWS = 32
+F8 = jnp.float8_e4m3fn
+LIFT = 256.0
+F8_MAX = 448.0
+SPAN = 32.0
+MODE_ROWS = 24
 CANDIDATES = 64
 
 
@@ -38,6 +42,12 @@
 def split(value):
     high = value.astype(BF16)
     return high, (value - high.astype(F32)).astype(BF16)
+
+
+def split_f8(value):
+    high = value.astype(BF16)
+    low = (value - high.astype(F32)) * LIFT
+    return high, jnp.clip(low, -F8_MAX, F8_MAX).astype(F8)
 
 
 def mm(left, right):
@@ -71,6 +81,8 @@
     upper_hot,
     m_high,
     m_low,
+    t_high,
+    t_low,
     mg_high,
     mg_low,
     p_ref,
@@ -79,6 +91,7 @@
     z_ref,
     base_ref,
     ab_ref,
+    ab_low,
     q_all,
     ghost_out,
     ghost_in,
@@ -132,7 +145,6 @@
 
     upper_hot[...] = hot(right, owned + halo, halo, q_row)
     wide = 256
-    broad = 1024
     tall_step = owned // 2
 
     @pl.loop(0, owned // wide)
@@ -142,9 +154,13 @@
         right_hot[pl.ds(at, wide), :] = right_now
         for part in range(owned // tall_step):
             r0 = part * tall_step
-            high, low = split(mm_nt(left_hot[r0 : r0 + tall_step, :], right_now))
+            block = mm_nt(left_hot[r0 : r0 + tall_step, :], right_now)
+            high, low = split_f8(block)
             m_high[r0 : r0 + tall_step, pl.ds(at, wide)] = high
             m_low[r0 : r0 + tall_step, pl.ds(at, wide)] = low
+            high, low = split_f8(block.T)
+            t_high[pl.ds(at, wide), r0 : r0 + tall_step] = high
+            t_low[pl.ds(at, wide), r0 : r0 + tall_step] = low
 
     def build_ghost_matrix():
         @pl.loop(0, owned // wide)
@@ -183,15 +199,20 @@
     gain_pad[...] = jnp.zeros((1, 128), F32)
     gain_pad[:, 0:modes] = gain_ref[...]
     send_row = jnp.concatenate([send_ref[0:1, :], send_ref[1:2, :]], axis=1)
-    sel_ref[...] = jnp.where(
+    sel_ref[:, 0 : 2 * halo] = jnp.where(
         send_row == lax.broadcasted_iota(jnp.int32, (owned, 2 * halo), 0), 1.0, 0.0
     ).astype(BF16)
+    pad = jnp.zeros((MODE_ROWS - modes, owned), F32)
+    lines = []
     for v in range(nvar):
-        shape_v = shapes_ref[v]
-        shape_v = jnp.concatenate([shape_v, jnp.zeros((MODE_ROWS - modes, owned), F32)], axis=0)
-        high, low = split(shape_v)
-        p_ref[v, 0:MODE_ROWS, :] = high
-        p_ref[v, MODE_ROWS:, :] = low
+        lines += [shapes_ref[v], pad]
+    lines.append(jnp.zeros((128 - nvar * MODE_ROWS, owned), F32))
+    high, low = split(jnp.concatenate(lines, axis=0))
+    p_ref[0:128, :] = high
+    p_ref[128:256, :] = low
+    sel_ref[:, 2 * halo : 2 * halo + 128] = high.astype(F32).T.astype(BF16)
+    sel_ref[:, 2 * halo + 128 :] = low.astype(F32).T.astype(BF16)
+    for v in range(nvar):
         z_ref[v * count : (v + 1) * count, :] = seed_ref[v]
     colours = col_ref[...]
 
@@ -205,23 +226,22 @@
             x_ref[spot, :] = jnp.where(mask, total, x_ref[spot, :])
 
     def coupling():
-        high, low = split(x_ref[...])
+        value = x_ref[...]
+        top = jnp.max(jnp.abs(value), axis=0, keepdims=True)
+        top = jnp.maximum(jnp.max(top, axis=1, keepdims=True), 1e-30)
+        scale = SPAN / top
+        high, low = split(value)
         both = mm(w_ref[...], jnp.concatenate([high, low, high], axis=0))
-        a_high, a_low = split(both[:rows])
-        b_high, b_low = split(both[rows : 2 * rows])
-        ab_ref[0, 0:rows, :] = a_high
-        ab_ref[0, rows:, :] = a_low
-        ab_ref[1, 0:rows, :] = b_high
-        ab_ref[1, rows:, :] = b_low
-        z_ref[...] = both[2 * rows :]
-
-        @pl.loop(0, owned // broad)
-        def _(t):
-            at = pl.multiple_of(t * broad, broad)
-            cols = pl.ds(at, broad)
-            one = mm(ab_ref[0], m_high[:, cols]) + mm_nt(ab_ref[1], m_high[cols, :])
-            two = mm(ab_ref[0, 0:rows, :], m_low[:, cols]) + mm_nt(ab_ref[1, 0:rows, :], m_low[cols, :])
-            z_ref[:, cols] = z_ref[:, cols] + (one[:rows] + one[rows:] + two)
+        for side in range(2):
+            part = both[side * rows : (side + 1) * rows]
+            high, low = split(part)
+            ab_ref[side, 0:rows, :] = high
+            ab_ref[side, rows:, :] = low
+            rough = jnp.concatenate([part * scale, jnp.zeros((96 - rows, owned), F32)], axis=0)
+            ab_low[side] = rough.astype(F8)
+        one = mm(ab_ref[0], m_high[...]) + mm(ab_ref[1], t_high[...])
+        two = mm(ab_low[0], m_low[...]) + mm(ab_low[1], t_low[...])
+        z_ref[...] = both[2 * rows :] + (one[:rows] + one[rows:] + two[:rows] * (top * (1.0 / (SPAN * LIFT))))
 
     def modal_copies(turn):
         return [
@@ -251,33 +271,30 @@
 
     def start_exchange(turn):
         high, low = split(x_ref[...])
-
-        @pl.when(turn < ITERS - 1)
-        def _():
-            picked = mm(jnp.concatenate([high, low], axis=0), sel_ref[...])
-            picked = picked[:rows] + picked[rows:]
-            ghost_out[turn, 0] = picked[:, :halo]
-            ghost_out[turn, 1] = picked[:, halo:]
-
-            @pl.when(turn == 0)
-            def _():
-                pl.semaphore_wait(barrier, n - 1)
-
-            for copy in ghost_copies(turn):
-                copy.start()
-
-        gram = jnp.zeros((2 * count, 2 * MODE_ROWS), F32)
-        for v in range(nvar):
-            spot = slice(v * count, (v + 1) * count)
-            gram = gram + mm_nt(jnp.concatenate([high[spot], low[spot]], axis=0), p_ref[v])
-        gram = gram[:count] + gram[count:]
-        part = gram[:, :MODE_ROWS] + gram[:, MODE_ROWS:]
+        every = mm(jnp.concatenate([high, low], axis=0), sel_ref[...])
+        every = every[:rows] + every[rows:]
+        gram = every[:, 2 * halo : 2 * halo + 128] + every[:, 2 * halo + 128 :]
+        part = gram[0:count, 0:MODE_ROWS]
+        for v in range(1, nvar):
+            part = part + gram[v * count : (v + 1) * count, v * MODE_ROWS : (v + 1) * MODE_ROWS]
         half = count // 2
         q_all[turn, me] = jnp.concatenate(
             [part[:half], part[half:], jnp.zeros((half, 128 - 2 * MODE_ROWS), F32)], axis=1
         )
+
+        @pl.when(turn == 0)
+        def _():
+            pl.semaphore_wait(barrier, n - 1)
+
         for copy in modal_copies(turn):
             copy.start()
+
+        @pl.when(turn < ITERS - 1)
+        def _():
+            ghost_out[turn, 0] = every[:, :halo]
+            ghost_out[turn, 1] = every[:, halo : 2 * halo]
+            for copy in ghost_copies(turn):
+                copy.start()
 
     def modal_sum(turn):
         total = q_all[turn, 0]
@@ -306,17 +323,22 @@
             high, low = split(jnp.concatenate([low_part, up_part], axis=1))
             both = mm(w_ref[0 : 2 * rows, :], jnp.concatenate([high, low, high], axis=0))
             ghost_ab = jnp.concatenate([both[:rows, :halo], both[rows:, halo:]], axis=1)
-            high, low = split(ghost_ab)
-            term = mm(jnp.concatenate([high, low], axis=0), mg_high[...])
-            term = term[:rows] + term[rows:] + mm(high, mg_low[...])
-            lam = modal_sum(sweep - 1)[:, :MODE_ROWS] * gain_pad[:, :MODE_ROWS]
+            ghost_high, ghost_low = split(ghost_ab)
+            lam = modal_sum(sweep - 1) * gain_pad[:, :MODE_ROWS]
+            lam = jnp.concatenate([lam] * nvar + [jnp.zeros((count, 128 - nvar * MODE_ROWS), F32)], axis=1)
+            lam = jnp.concatenate([lam] * nvar, axis=0)
+            lane = lax.broadcasted_iota(jnp.int32, (rows, 128), 1)
+            line = lax.broadcasted_iota(jnp.int32, (rows, 128), 0)
+            lam = jnp.where(lax.div(lane, MODE_ROWS) == lax.div(line, count), -lam, 0.0)
             lam_high, lam_low = split(lam)
-            lam_both = jnp.concatenate([lam_high, lam_low], axis=0)
+            term = mm(jnp.concatenate([ghost_high, ghost_low], axis=0), mg_high[...]) + mm(
+                jnp.concatenate([lam_high, lam_low], axis=0), p_ref[0:128, :]
+            )
+            rest = mm(ghost_high, mg_low[...]) + mm(lam_high, p_ref[128:256, :])
+            term = term[:rows] + term[rows:] + rest
             for v in range(nvar):
                 spot = slice(v * count, (v + 1) * count)
-                lift = mm(lam_both, p_ref[v, 0:MODE_ROWS, :])
-                lift = lift[:count] + lift[count:] + mm(lam_high, p_ref[v, MODE_ROWS:, :])
-                base = seed_ref[v] + lift - term[spot]
+                base = seed_ref[v] - term[spot]
                 base_ref[spot, :] = base
                 z_ref[spot, :] = base - z_ref[spot, :]
 
@@ -406,15 +428,18 @@
             pltpu.VMEM((owned, nfaces), BF16),
             pltpu.VMEM((halo, nfaces), BF16),
             pltpu.VMEM((owned, owned), BF16),
+            pltpu.VMEM((owned, owned), F8),
             pltpu.VMEM((owned, owned), BF16),
+            pltpu.VMEM((owned, owned), F8),
             pltpu.VMEM((2 * halo, owned), BF16),
             pltpu.VMEM((2 * halo, owned), BF16),
-            pltpu.VMEM((nvar, 2 * MODE_ROWS, owned), BF16),
-            pltpu.VMEM((owned, 2 * halo), BF16),
+            pltpu.VMEM((256, owned), BF16),
+            pltpu.VMEM((owned, 2 * halo + 256), BF16),
             pltpu.VMEM((rows, owned), F32),
             pltpu.VMEM((rows, owned), F32),
             pltpu.VMEM((rows, owned), F32),
             pltpu.VMEM((2, 2 * rows, owned), BF16),
+            pltpu.VMEM((2, 96, owned), F8),
             pltpu.VMEM((turns, n, count // 2, 128), F32),
             pltpu.VMEM((turns - 1, 2, rows, halo), F32),
             pltpu.VMEM((turns - 1, 2, rows, halo), F32),

time: 52.7 us -> 47.4 us (0.90)
  Pallas kernels: 51.8 us -> 46.6 us
    pallas_call x1, Pallas kernels: 50.1 us -> 44.9 us  [local(): pl.pallas_call(functools.partial(kernel, n), out_shape=(jax.ShapeDtypeStr...]
where the time goes in v3:
time: 47.4 us; the launch traced here: 47.2 us
  Pallas kernels  46.6 us (98%)
  between operations  0.64 us (1%)
    pallas_call x1, Pallas kernels, local(): pl.pallas_call(functools.partial(kernel, n), out_shape=(jax.ShapeDtypeStr...  44.9 us
    pallas_call x1, Pallas kernels, local(): pl.pallas_call(hand_over, out_shape=(jax.ShapeDtypeStruct((rows, owned),...  1.7 us

profile of v3, /device:TPU:0, one launch (start us, length us, event | category | flops | bytes accessed | tf_op | source)
XLA Modules:
  0.0 47.2 jit_solution(4656241002048700413)
XLA Ops:
  0.6 44.9 %shard_map.104 = (f32[80,1024]{1,0:T(8,128)}, f32[16,20]{1,0:T(8,128)}) custom-call(f32[5,16,1024]{2,1,0:T(8,128)} %bitcast.12, bf16[5,5,16,1024]{3,2,1,0:T(8,128)(2,1)} %bitcast.10, f32[5,5,2,16]{3,2,1,0:T(2,128)} %bitcast.13, f32[5,20,1024]{2,1,0:T(8,128)} %bitcast.11, f32[1,20]{1,0:T(1,128)} %bitcast.16, s32[2,3072]{1,0:T(2,128)} %faces_ref.1, ...), custom_call_target="tpu_custom_call" | custom-call | tf_op jit(solution)/shard_map/pallas_call | solution.py:413
  45.5 1.7 %shard_map.105 = (f32[80,1024]{1,0:T(8,128)}, f32[16,20]{1,0:T(8,128)}) custom-call(f32[80,1024]{1,0:T(8,128)} %get-tuple-element.6.out_ref, f32[16,20]{1,0:T(8,128)} %get-tuple-element.7.part_ref), custom_call_target="tpu_custom_call" | custom-call | tf_op jit(solution)/shard_map/pallas_call | solution.py:466

commit v4 on v3

--- a/solution.py
+++ b/solution.py
@@ -79,6 +79,8 @@
     left_hot,
     right_hot,
     upper_hot,
+    index_rows,
+    value_rows,
     m_high,
     m_low,
     t_high,
@@ -131,26 +133,55 @@
     step = 128
     tall = owned + halo
 
-    def hot(index, start, size, value):
-        lines = lax.broadcasted_iota(jnp.int32, (size, 128), 0).astype(jnp.int16)
-        lines = jnp.concatenate([lines] * (nfaces // 128), axis=1)
-        near = jnp.broadcast_to((index.astype(jnp.int32) - start).astype(jnp.int16), (size, nfaces))
-        zero = jnp.zeros((size, nfaces), BF16)
-        return jnp.where(near == lines, jnp.broadcast_to(value, (size, nfaces)), zero)
+    for k, row in enumerate((left, right)):
+        index_rows[k] = jnp.broadcast_to(row, (16, nfaces))
+    for k, row in enumerate((p_row, q_row)):
+        value_rows[k] = jnp.broadcast_to(row, (16, nfaces))
+    sixteen = lax.broadcasted_iota(jnp.int32, (16, 128), 0)
+
+    def hot(side, start, size):
+        near = index_rows[side]
+        value = value_rows[side]
+        zero = jnp.zeros((16, nfaces), BF16)
+        strips = []
+        for k in range(size // 16):
+            line = (sixteen + (start + 16 * k)).astype(jnp.int16)
+            strips.append(jnp.where(near == jnp.concatenate([line] * (nfaces // 128), axis=1), value, zero))
+        return jnp.concatenate(strips, axis=0)
 
     @pl.loop(0, tall // step)
     def _(t):
         at = pl.multiple_of(t * step, step)
-        left_hot[pl.ds(at, step), :] = hot(left, at, step, p_row)
-
-    upper_hot[...] = hot(right, owned + halo, halo, q_row)
+        left_hot[pl.ds(at, step), :] = hot(0, at, step)
+
+    upper_hot[...] = hot(1, owned + halo, halo)
     wide = 256
     tall_step = owned // 2
+
+    send_row = jnp.concatenate([send_ref[0:1, :], send_ref[1:2, :]], axis=1)
+    for load in loads:
+        load.wait()
 
     @pl.loop(0, owned // wide)
     def _(t):
         at = pl.multiple_of(t * wide, wide)
-        right_now = hot(right, at, wide, q_row)
+        here = pl.ds(at, wide)
+        sel_ref[here, 0 : 2 * halo] = jnp.where(
+            send_row - at == lax.broadcasted_iota(jnp.int32, (wide, 2 * halo), 0), 1.0, 0.0
+        ).astype(BF16)
+        pad = jnp.zeros((MODE_ROWS - modes, wide), F32)
+        lines = []
+        for v in range(nvar):
+            lines += [shapes_ref[v, :, here], pad]
+            z_ref[v * count : (v + 1) * count, here] = seed_ref[v, :, here]
+            base_ref[v * count : (v + 1) * count, here] = seed_ref[v, :, here]
+        lines.append(jnp.zeros((128 - nvar * MODE_ROWS, wide), F32))
+        high, low = split(jnp.concatenate(lines, axis=0))
+        p_ref[0:128, here] = high
+        p_ref[128:256, here] = low
+        sel_ref[here, 2 * halo : 2 * halo + 128] = high.astype(F32).T.astype(BF16)
+        sel_ref[here, 2 * halo + 128 :] = low.astype(F32).T.astype(BF16)
+        right_now = hot(1, at, wide)
         right_hot[pl.ds(at, wide), :] = right_now
         for part in range(owned // tall_step):
             r0 = part * tall_step
@@ -194,26 +225,8 @@
     first = jnp.where((lane == line) | (lane == line + rows), 1.0, 0.0).astype(BF16)
     last = jnp.where(lane == line + 2 * rows, 1.0, 0.0).astype(BF16)
     w_ref[...] = (mm(w_high, first) + mm(w_low, last)).astype(BF16)
-    for load in loads:
-        load.wait()
     gain_pad[...] = jnp.zeros((1, 128), F32)
     gain_pad[:, 0:modes] = gain_ref[...]
-    send_row = jnp.concatenate([send_ref[0:1, :], send_ref[1:2, :]], axis=1)
-    sel_ref[:, 0 : 2 * halo] = jnp.where(
-        send_row == lax.broadcasted_iota(jnp.int32, (owned, 2 * halo), 0), 1.0, 0.0
-    ).astype(BF16)
-    pad = jnp.zeros((MODE_ROWS - modes, owned), F32)
-    lines = []
-    for v in range(nvar):
-        lines += [shapes_ref[v], pad]
-    lines.append(jnp.zeros((128 - nvar * MODE_ROWS, owned), F32))
-    high, low = split(jnp.concatenate(lines, axis=0))
-    p_ref[0:128, :] = high
-    p_ref[128:256, :] = low
-    sel_ref[:, 2 * halo : 2 * halo + 128] = high.astype(F32).T.astype(BF16)
-    sel_ref[:, 2 * halo + 128 :] = low.astype(F32).T.astype(BF16)
-    for v in range(nvar):
-        z_ref[v * count : (v + 1) * count, :] = seed_ref[v]
     colours = col_ref[...]
 
     def update(colour):
@@ -248,13 +261,18 @@
             pltpu.make_async_remote_copy(
                 src_ref=q_all.at[turn, me],
                 dst_ref=q_all.at[turn, me],
-                send_sem=q_send.at[turn, d],
-                recv_sem=q_recv.at[turn, d],
+                send_sem=q_send.at[turn],
+                recv_sem=q_recv.at[turn],
                 device_id={"cell": peers[d]},
                 device_id_type=pl.DeviceIdType.MESH,
             )
             for d in range(n - 1, 0, -1)
         ]
+
+    def wait_modal(turn):
+        every = q_all.at[turn, pl.ds(0, n - 1)]
+        pltpu.make_async_copy(every, every, q_send.at[turn]).wait()
+        pltpu.make_async_copy(every, every, q_recv.at[turn]).wait()
 
     def ghost_copies(turn):
         return [
@@ -303,9 +321,6 @@
         return jnp.concatenate([total[:, :MODE_ROWS], total[:, MODE_ROWS : 2 * MODE_ROWS]], axis=0)
 
     x_ref[...] = jnp.zeros((rows, owned), F32)
-    for v in range(nvar):
-        base_ref[v * count : (v + 1) * count, :] = seed_ref[v]
-
     @pl.loop(0, ITERS)
     def _(sweep):
         @pl.when(sweep > 0)
@@ -316,8 +331,9 @@
             def _():
                 build_ghost_matrix()
 
-            for copy in ghost_copies(sweep - 1) + modal_copies(sweep - 1):
+            for copy in ghost_copies(sweep - 1):
                 copy.wait()
+            wait_modal(sweep - 1)
             low_part = ghost_in[sweep - 1, 0]
             up_part = ghost_in[sweep - 1, 1]
             high, low = split(jnp.concatenate([low_part, up_part], axis=1))
@@ -350,8 +366,7 @@
 
     store = pltpu.make_async_copy(x_ref, out_hbm, in_sem.at[0])
     store.start()
-    for copy in modal_copies(ITERS - 1):
-        copy.wait()
+    wait_modal(ITERS - 1)
     part_ref[...] = modal_sum(ITERS - 1)[:, :modes]
     store.wait()
 
@@ -427,6 +442,8 @@
             pltpu.VMEM((tall, nfaces), BF16),
             pltpu.VMEM((owned, nfaces), BF16),
             pltpu.VMEM((halo, nfaces), BF16),
+            pltpu.VMEM((2, 16, nfaces), jnp.int16),
+            pltpu.VMEM((2, 16, nfaces), BF16),
             pltpu.VMEM((owned, owned), BF16),
             pltpu.VMEM((owned, owned), F8),
             pltpu.VMEM((owned, owned), BF16),
@@ -444,8 +461,8 @@
             pltpu.VMEM((turns - 1, 2, rows, halo), F32),
             pltpu.VMEM((turns - 1, 2, rows, halo), F32),
             pltpu.SemaphoreType.DMA((3,)),
-            pltpu.SemaphoreType.DMA((turns, n)),
-            pltpu.SemaphoreType.DMA((turns, n)),
+            pltpu.SemaphoreType.DMA((turns,)),
+            pltpu.SemaphoreType.DMA((turns,)),
             pltpu.SemaphoreType.DMA((turns - 1, 2)),
             pltpu.SemaphoreType.DMA((turns - 1, 2)),
         ],

time: 47.4 us -> 45.9 us (0.968)
  Pallas kernels: 46.6 us -> 45 us
    pallas_call x1, Pallas kernels: 44.9 us -> 43.3 us  [local(): pl.pallas_call(functools.partial(kernel, n), out_shape=(jax.ShapeDtypeStr...]
where the time goes in v4:
time: 45.9 us; the launch traced here: 45.7 us
  Pallas kernels  45 us (98%)
  between operations  0.64 us (1%)
    pallas_call x1, Pallas kernels, local(): pl.pallas_call(functools.partial(kernel, n), out_shape=(jax.ShapeDtypeStr...  43.3 us
    pallas_call x1, Pallas kernels, local(): pl.pallas_call(hand_over, out_shape=(jax.ShapeDtypeStruct((rows, owned),...  1.7 us

profile of v4, /device:TPU:0, one launch (start us, length us, event | category | flops | bytes accessed | tf_op | source)
XLA Modules:
  0.0 45.7 jit_solution(12253323016557802701)
XLA Ops:
  0.6 43.3 %shard_map.104 = (f32[80,1024]{1,0:T(8,128)}, f32[16,20]{1,0:T(8,128)}) custom-call(f32[5,16,1024]{2,1,0:T(8,128)} %bitcast.12, bf16[5,5,16,1024]{3,2,1,0:T(8,128)(2,1)} %bitcast.10, f32[5,5,2,16]{3,2,1,0:T(2,128)} %bitcast.13, f32[5,20,1024]{2,1,0:T(8,128)} %bitcast.11, f32[1,20]{1,0:T(1,128)} %bitcast.16, s32[2,3072]{1,0:T(2,128)} %faces_ref.1, ...), custom_call_target="tpu_custom_call" | custom-call | tf_op jit(solution)/shard_map/pallas_call | solution.py:428
  44.0 1.7 %shard_map.105 = (f32[80,1024]{1,0:T(8,128)}, f32[16,20]{1,0:T(8,128)}) custom-call(f32[80,1024]{1,0:T(8,128)} %get-tuple-element.6.out_ref, f32[16,20]{1,0:T(8,128)} %get-tuple-element.7.part_ref), custom_call_target="tpu_custom_call" | custom-call | tf_op jit(solution)/shard_map/pallas_call | solution.py:483

commit v5 on v4

--- a/solution.py
+++ b/solution.py
@@ -77,8 +77,9 @@
     w_ref,
     gain_pad,
     left_hot,
-    right_hot,
     upper_hot,
+    block_a,
+    block_b,
     index_rows,
     value_rows,
     m_high,
@@ -131,6 +132,8 @@
     p_row = jnp.concatenate([p_tile[k : k + 1, :] for k in range(nfaces // 128)], axis=1).astype(BF16)
     q_row = jnp.concatenate([q_tile[k : k + 1, :] for k in range(nfaces // 128)], axis=1).astype(BF16)
     step = 128
+    wide = 256
+    tall_step = owned // 2
     tall = owned + halo
 
     for k, row in enumerate((left, right)):
@@ -149,21 +152,35 @@
             strips.append(jnp.where(near == jnp.concatenate([line] * (nfaces // 128), axis=1), value, zero))
         return jnp.concatenate(strips, axis=0)
 
+    blocks_ref = (block_a, block_b)
+
+    def split_block(at, slot):
+        here = pl.ds(at, wide)
+        for part in range(owned // tall_step):
+            r0 = part * tall_step
+            block = blocks_ref[slot][r0 : r0 + tall_step, :]
+            high, low = split_f8(block)
+            m_high[r0 : r0 + tall_step, here] = high
+            m_low[r0 : r0 + tall_step, here] = low
+            high, low = split_f8(block.T)
+            t_high[here, r0 : r0 + tall_step] = high
+            t_low[here, r0 : r0 + tall_step] = low
+        high, low = split(blocks_ref[slot][owned:tall, :])
+        mg_high[0:halo, here] = high
+        mg_low[0:halo, here] = low
+
     @pl.loop(0, tall // step)
     def _(t):
         at = pl.multiple_of(t * step, step)
         left_hot[pl.ds(at, step), :] = hot(0, at, step)
 
     upper_hot[...] = hot(1, owned + halo, halo)
-    wide = 256
-    tall_step = owned // 2
 
     send_row = jnp.concatenate([send_ref[0:1, :], send_ref[1:2, :]], axis=1)
     for load in loads:
         load.wait()
 
-    @pl.loop(0, owned // wide)
-    def _(t):
+    def build_tile(t, slot):
         at = pl.multiple_of(t * wide, wide)
         here = pl.ds(at, wide)
         sel_ref[here, 0 : 2 * halo] = jnp.where(
@@ -182,24 +199,23 @@
         sel_ref[here, 2 * halo : 2 * halo + 128] = high.astype(F32).T.astype(BF16)
         sel_ref[here, 2 * halo + 128 :] = low.astype(F32).T.astype(BF16)
         right_now = hot(1, at, wide)
-        right_hot[pl.ds(at, wide), :] = right_now
-        for part in range(owned // tall_step):
-            r0 = part * tall_step
-            block = mm_nt(left_hot[r0 : r0 + tall_step, :], right_now)
-            high, low = split_f8(block)
-            m_high[r0 : r0 + tall_step, pl.ds(at, wide)] = high
-            m_low[r0 : r0 + tall_step, pl.ds(at, wide)] = low
-            high, low = split_f8(block.T)
-            t_high[pl.ds(at, wide), r0 : r0 + tall_step] = high
-            t_low[pl.ds(at, wide), r0 : r0 + tall_step] = low
+        earlier = lax.rem(t + owned // wide - 1, owned // wide)
+        split_block(pl.multiple_of(earlier * wide, wide), 1 - slot)
+        for part in range(2):
+            r0 = part * (tall // 2)
+            blocks_ref[slot][r0 : r0 + tall // 2, :] = mm_nt(left_hot[r0 : r0 + tall // 2, :], right_now)
+
+    @pl.loop(0, owned // (2 * wide))
+    def _(t):
+        build_tile(2 * t, 0)
+        build_tile(2 * t + 1, 1)
+
+    split_block(owned - wide, (owned // wide - 1) % 2)
 
     def build_ghost_matrix():
         @pl.loop(0, owned // wide)
         def _(t):
             at = pl.multiple_of(t * wide, wide)
-            high, low = split(mm_nt(left_hot[owned:tall, :], right_hot[pl.ds(at, wide), :]))
-            mg_high[0:halo, pl.ds(at, wide)] = high
-            mg_low[0:halo, pl.ds(at, wide)] = low
             high, low = split(mm_nt(upper_hot[...], left_hot[pl.ds(at, wide), :]))
             mg_high[halo:, pl.ds(at, wide)] = high
             mg_low[halo:, pl.ds(at, wide)] = low
@@ -364,11 +380,9 @@
         update(1)
         start_exchange(sweep)
 
-    store = pltpu.make_async_copy(x_ref, out_hbm, in_sem.at[0])
-    store.start()
+    out_hbm[...] = x_ref[...]
     wait_modal(ITERS - 1)
     part_ref[...] = modal_sum(ITERS - 1)[:, :modes]
-    store.wait()
 
 
 def partners(me, n):
@@ -386,21 +400,13 @@
     return places
 
 
-def hand_over(out_ref, part_ref, out_final, part_final, stage, small, sem):
-    pieces = 5
-    size = out_ref.shape[0] // pieces
-    spots = [pl.ds(k * size, size) for k in range(pieces)]
-    ins = [pltpu.make_async_copy(out_ref.at[s], stage.at[s], sem.at[0, k]) for k, s in enumerate(spots)]
-    outs = [pltpu.make_async_copy(stage.at[s], out_final.at[s], sem.at[1, k]) for k, s in enumerate(spots)]
-    ins.append(pltpu.make_async_copy(part_ref, small, sem.at[0, pieces]))
-    outs.append(pltpu.make_async_copy(small, part_final, sem.at[1, pieces]))
-    for copy in ins:
-        copy.start()
-    for first, second in zip(ins, outs):
-        first.wait()
-        second.start()
-    for copy in outs:
-        copy.wait()
+def hand_over(out_ref, part_ref, out_final, part_final, sem):
+    first = pltpu.make_async_copy(out_ref, out_final, sem.at[0])
+    second = pltpu.make_async_copy(part_ref, part_final, sem.at[1])
+    first.start()
+    second.start()
+    first.wait()
+    second.wait()
 
 
 def local(
@@ -428,11 +434,11 @@
     out, part = pl.pallas_call(
         functools.partial(kernel, n),
         out_shape=(
-            jax.ShapeDtypeStruct((rows, owned), F32),
-            jax.ShapeDtypeStruct((count, modes), F32),
+            pltpu.VMEM((rows, owned), F32),
+            pltpu.VMEM((count, modes), F32),
         ),
         in_specs=[hbm, hbm, vmem, hbm] + [vmem] * 5,
-        out_specs=(hbm, vmem),
+        out_specs=(vmem, vmem),
         scratch_shapes=[
             pltpu.VMEM((nvar, count, owned), F32),
             pltpu.VMEM((nvar, nvar, count, owned), BF16),
@@ -440,8 +446,9 @@
             pltpu.VMEM((3 * rows, 3 * rows), BF16),
             pltpu.VMEM((1, 128), F32),
             pltpu.VMEM((tall, nfaces), BF16),
-            pltpu.VMEM((owned, nfaces), BF16),
             pltpu.VMEM((halo, nfaces), BF16),
+            pltpu.VMEM((tall, 256), F32),
+            pltpu.VMEM((tall, 256), F32),
             pltpu.VMEM((2, 16, nfaces), jnp.int16),
             pltpu.VMEM((2, 16, nfaces), BF16),
             pltpu.VMEM((owned, owned), BF16),
@@ -486,14 +493,15 @@
             jax.ShapeDtypeStruct((rows, owned), F32),
             jax.ShapeDtypeStruct((count, modes), F32),
         ),
-        in_specs=[hbm, hbm],
+        in_specs=[vmem, vmem],
         out_specs=(hbm, hbm),
         scratch_shapes=[
-            pltpu.VMEM((rows, owned), F32),
-            pltpu.VMEM((count, modes), F32),
-            pltpu.SemaphoreType.DMA((2, 6)),
+            pltpu.SemaphoreType.DMA((2,)),
         ],
-    )(out, part)
+    )(
+        pltpu.with_memory_space_constraint(out, pltpu.VMEM),
+        pltpu.with_memory_space_constraint(part, pltpu.VMEM),
+    )
     return jnp.transpose(out.reshape(nvar, count, owned), (1, 0, 2)), part
 
 

time: 45.9 us -> 42.7 us (0.930)
  Pallas kernels: 45 us -> 41.9 us
    pallas_call x1, Pallas kernels: 43.3 us -> 41.1 us  [local(): pl.pallas_call(functools.partial(kernel, n), out_shape=(pltpu.VMEM((rows,...]
    pallas_call x1, Pallas kernels: 1.7 us -> 0.75 us  [local(): pl.pallas_call(hand_over, out_shape=(jax.ShapeDtypeStruct((rows, owned),...]
where the time goes in v5:
time: 42.7 us; the launch traced here: 42.5 us
  Pallas kernels  41.9 us (98%)
  between operations  0.64 us (1%)
    pallas_call x1, Pallas kernels, local(): pl.pallas_call(functools.partial(kernel, n), out_shape=(pltpu.VMEM((rows,...  41.1 us

profile of v5, /device:TPU:0, one launch (start us, length us, event | category | flops | bytes accessed | tf_op | source)
XLA Modules:
  0.0 42.5 jit_solution(18143687544844163617)
XLA Ops:
  0.6 41.1 %shard_map.104 = (f32[80,1024]{1,0:T(8,128)S(1)}, f32[16,20]{1,0:T(8,128)S(1)}) custom-call(f32[5,16,1024]{2,1,0:T(8,128)} %bitcast.12, bf16[5,5,16,1024]{3,2,1,0:T(8,128)(2,1)} %bitcast.10, f32[5,5,2,16]{3,2,1,0:T(2,128)} %bitcast.13, f32[5,20,1024]{2,1,0:T(8,128)} %bitcast.11, f32[1,20]{1,0:T(1,128)} %bitcast.16, s32[2,3072]{1,0:T(2,128)} %faces_ref.1, ...), custom_call_target="tpu_custom_call" | custom-call | tf_op jit(solution)/shard_map/pallas_call | solution.py:434
  41.8 0.7 %shard_map.105 = (f32[80,1024]{1,0:T(8,128)}, f32[16,20]{1,0:T(8,128)}) custom-call(f32[80,1024]{1,0:T(8,128)S(1)} %get-tuple-element.6.out_ref, f32[16,20]{1,0:T(8,128)S(1)} %get-tuple-element.7.part_ref), custom_call_target="tpu_custom_call" | custom-call | tf_op jit(solution)/shard_map/pallas_call | solution.py:490

commit v6 on v5

--- a/solution.py
+++ b/solution.py
@@ -17,7 +17,7 @@
 F8_MAX = 448.0
 SPAN = 32.0
 MODE_ROWS = 24
-CANDIDATES = 64
+CANDIDATES = 40
 
 
 def spectral_weights(count):
@@ -25,18 +25,14 @@
 
 
 def bf16_factors(value):
-    best_p = value.astype(BF16).astype(F32)
     best_q = jnp.ones_like(value)
-    best = jnp.abs(value - best_p)
+    best = jnp.abs(value - value.astype(BF16).astype(F32))
     for k in range(1, CANDIDATES):
         q = 1.0 + k / 128.0
-        p = (value * (1.0 / q)).astype(BF16).astype(F32)
-        miss = jnp.abs(value - p * q)
-        better = miss < best
-        best = jnp.where(better, miss, best)
-        best_p = jnp.where(better, p, best_p)
-        best_q = jnp.where(better, q, best_q)
-    return best_p.astype(BF16), best_q.astype(BF16)
+        miss = jnp.abs(value - (value * (1.0 / q)).astype(BF16).astype(F32) * q)
+        best_q = jnp.where(miss < best, q, best_q)
+        best = jnp.minimum(miss, best)
+    return (value / best_q).astype(BF16), best_q.astype(BF16)
 
 
 def split(value):
@@ -133,7 +129,6 @@
     q_row = jnp.concatenate([q_tile[k : k + 1, :] for k in range(nfaces // 128)], axis=1).astype(BF16)
     step = 128
     wide = 256
-    tall_step = owned // 2
     tall = owned + halo
 
     for k, row in enumerate((left, right)):
@@ -152,35 +147,30 @@
             strips.append(jnp.where(near == jnp.concatenate([line] * (nfaces // 128), axis=1), value, zero))
         return jnp.concatenate(strips, axis=0)
 
-    blocks_ref = (block_a, block_b)
-
-    def split_block(at, slot):
+    cut = owned // 2
+
+    def split_block(at, block_ref, r0, r1):
         here = pl.ds(at, wide)
-        for part in range(owned // tall_step):
-            r0 = part * tall_step
-            block = blocks_ref[slot][r0 : r0 + tall_step, :]
-            high, low = split_f8(block)
-            m_high[r0 : r0 + tall_step, here] = high
-            m_low[r0 : r0 + tall_step, here] = low
-            high, low = split_f8(block.T)
-            t_high[here, r0 : r0 + tall_step] = high
-            t_low[here, r0 : r0 + tall_step] = low
-        high, low = split(blocks_ref[slot][owned:tall, :])
-        mg_high[0:halo, here] = high
-        mg_low[0:halo, here] = low
+        block = block_ref[0 : r1 - r0, :]
+        high, low = split_f8(block)
+        m_high[r0:r1, here] = high
+        m_low[r0:r1, here] = low
+        high, low = split_f8(block.T)
+        t_high[here, r0:r1] = high
+        t_low[here, r0:r1] = low
 
     @pl.loop(0, tall // step)
     def _(t):
         at = pl.multiple_of(t * step, step)
         left_hot[pl.ds(at, step), :] = hot(0, at, step)
 
-    upper_hot[...] = hot(1, owned + halo, halo)
 
     send_row = jnp.concatenate([send_ref[0:1, :], send_ref[1:2, :]], axis=1)
-    for load in loads:
-        load.wait()
-
-    def build_tile(t, slot):
+    loads[0].wait()
+    loads[1].wait()
+
+    @pl.loop(0, owned // wide)
+    def _(t):
         at = pl.multiple_of(t * wide, wide)
         here = pl.ds(at, wide)
         sel_ref[here, 0 : 2 * halo] = jnp.where(
@@ -198,21 +188,42 @@
         p_ref[128:256, here] = low
         sel_ref[here, 2 * halo : 2 * halo + 128] = high.astype(F32).T.astype(BF16)
         sel_ref[here, 2 * halo + 128 :] = low.astype(F32).T.astype(BF16)
+        eye_line = lax.broadcasted_iota(jnp.int32, (count, rows), 0)
+        eye_lane = lax.broadcasted_iota(jnp.int32, (count, rows), 1)
+        eye = lax.rem(eye_lane, count) == eye_line
+        blocks = []
+        for side in range(2):
+            for w in range(nvar):
+                row = jnp.concatenate([flux_ref[v, w][side : side + 1, :] for v in range(nvar)], axis=1)
+                blocks.append(jnp.where(eye, jnp.broadcast_to(row, (count, rows)), 0.0))
+        line = lax.broadcasted_iota(jnp.int32, (rows, rows), 0)
+        lane = lax.broadcasted_iota(jnp.int32, (rows, rows), 1)
+        apart = lax.rem(lane, count) - lax.rem(line, count)
+        spectral = jnp.zeros((rows, rows), F32)
+        for d, weight in enumerate(spectral_weights(count), 1):
+            spectral = jnp.where(apart == d, weight, jnp.where(apart == -d, -weight, spectral))
+        spectral = jnp.where(lax.div(lane, count) == lax.div(line, count), spectral, 0.0)
+        w_high, w_low = split(jnp.concatenate(blocks + [spectral], axis=0))
+        lane = lax.broadcasted_iota(jnp.int32, (rows, 3 * rows), 1)
+        line = lax.broadcasted_iota(jnp.int32, (rows, 3 * rows), 0)
+        first = jnp.where((lane == line) | (lane == line + rows), 1.0, 0.0).astype(BF16)
+        last = jnp.where(lane == line + 2 * rows, 1.0, 0.0).astype(BF16)
+        w_ref[...] = (mm(w_high, first) + mm(w_low, last)).astype(BF16)
         right_now = hot(1, at, wide)
         earlier = lax.rem(t + owned // wide - 1, owned // wide)
-        split_block(pl.multiple_of(earlier * wide, wide), 1 - slot)
-        for part in range(2):
-            r0 = part * (tall // 2)
-            blocks_ref[slot][r0 : r0 + tall // 2, :] = mm_nt(left_hot[r0 : r0 + tall // 2, :], right_now)
-
-    @pl.loop(0, owned // (2 * wide))
-    def _(t):
-        build_tile(2 * t, 0)
-        build_tile(2 * t + 1, 1)
-
-    split_block(owned - wide, (owned // wide - 1) % 2)
+        split_block(pl.multiple_of(earlier * wide, wide), block_b, 0, cut)
+        block_a[...] = mm_nt(left_hot[cut:tall, :], right_now)
+        split_block(at, block_a, cut, owned)
+        high, low = split(block_a[owned - cut : tall - cut, :])
+        mg_high[0:halo, here] = high
+        mg_low[0:halo, here] = low
+        block_b[...] = mm_nt(left_hot[0:cut, :], right_now)
+
+    split_block(owned - wide, block_b, 0, cut)
 
     def build_ghost_matrix():
+        upper_hot[...] = hot(1, owned + halo, halo)
+
         @pl.loop(0, owned // wide)
         def _(t):
             at = pl.multiple_of(t * wide, wide)
@@ -220,27 +231,7 @@
             mg_high[halo:, pl.ds(at, wide)] = high
             mg_low[halo:, pl.ds(at, wide)] = low
 
-    eye_line = lax.broadcasted_iota(jnp.int32, (count, rows), 0)
-    eye_lane = lax.broadcasted_iota(jnp.int32, (count, rows), 1)
-    eye = lax.rem(eye_lane, count) == eye_line
-    blocks = []
-    for side in range(2):
-        for w in range(nvar):
-            row = jnp.concatenate([flux_ref[v, w][side : side + 1, :] for v in range(nvar)], axis=1)
-            blocks.append(jnp.where(eye, jnp.broadcast_to(row, (count, rows)), 0.0))
-    line = lax.broadcasted_iota(jnp.int32, (rows, rows), 0)
-    lane = lax.broadcasted_iota(jnp.int32, (rows, rows), 1)
-    apart = lax.rem(lane, count) - lax.rem(line, count)
-    spectral = jnp.zeros((rows, rows), F32)
-    for d, weight in enumerate(spectral_weights(count), 1):
-        spectral = jnp.where(apart == d, weight, jnp.where(apart == -d, -weight, spectral))
-    spectral = jnp.where(lax.div(lane, count) == lax.div(line, count), spectral, 0.0)
-    w_high, w_low = split(jnp.concatenate(blocks + [spectral], axis=0))
-    lane = lax.broadcasted_iota(jnp.int32, (rows, 3 * rows), 1)
-    line = lax.broadcasted_iota(jnp.int32, (rows, 3 * rows), 0)
-    first = jnp.where((lane == line) | (lane == line + rows), 1.0, 0.0).astype(BF16)
-    last = jnp.where(lane == line + 2 * rows, 1.0, 0.0).astype(BF16)
-    w_ref[...] = (mm(w_high, first) + mm(w_low, last)).astype(BF16)
+    loads[2].wait()
     gain_pad[...] = jnp.zeros((1, 128), F32)
     gain_pad[:, 0:modes] = gain_ref[...]
     colours = col_ref[...]
@@ -307,21 +298,9 @@
         high, low = split(x_ref[...])
         every = mm(jnp.concatenate([high, low], axis=0), sel_ref[...])
         every = every[:rows] + every[rows:]
-        gram = every[:, 2 * halo : 2 * halo + 128] + every[:, 2 * halo + 128 :]
-        part = gram[0:count, 0:MODE_ROWS]
-        for v in range(1, nvar):
-            part = part + gram[v * count : (v + 1) * count, v * MODE_ROWS : (v + 1) * MODE_ROWS]
-        half = count // 2
-        q_all[turn, me] = jnp.concatenate(
-            [part[:half], part[half:], jnp.zeros((half, 128 - 2 * MODE_ROWS), F32)], axis=1
-        )
-
         @pl.when(turn == 0)
         def _():
             pl.semaphore_wait(barrier, n - 1)
-
-        for copy in modal_copies(turn):
-            copy.start()
 
         @pl.when(turn < ITERS - 1)
         def _():
@@ -330,11 +309,21 @@
             for copy in ghost_copies(turn):
                 copy.start()
 
+        gram = every[:, 2 * halo : 2 * halo + 128] + every[:, 2 * halo + 128 :]
+        part = gram[0:count, 0:MODE_ROWS]
+        for v in range(1, nvar):
+            part = part + gram[v * count : (v + 1) * count, v * MODE_ROWS : (v + 1) * MODE_ROWS]
+        size = count // 4
+        pieces = [part[k * size : (k + 1) * size] for k in range(4)]
+        q_all[turn, me] = jnp.concatenate(pieces + [jnp.zeros((size, 128 - 4 * MODE_ROWS), F32)], axis=1)
+        for copy in modal_copies(turn):
+            copy.start()
+
     def modal_sum(turn):
         total = q_all[turn, 0]
         for d in range(1, n):
             total = total + q_all[turn, d]
-        return jnp.concatenate([total[:, :MODE_ROWS], total[:, MODE_ROWS : 2 * MODE_ROWS]], axis=0)
+        return jnp.concatenate([total[:, k * MODE_ROWS : (k + 1) * MODE_ROWS] for k in range(4)], axis=0)
 
     x_ref[...] = jnp.zeros((rows, owned), F32)
     @pl.loop(0, ITERS)
@@ -447,8 +436,8 @@
             pltpu.VMEM((1, 128), F32),
             pltpu.VMEM((tall, nfaces), BF16),
             pltpu.VMEM((halo, nfaces), BF16),
-            pltpu.VMEM((tall, 256), F32),
-            pltpu.VMEM((tall, 256), F32),
+            pltpu.VMEM((owned // 2 + halo, 256), F32),
+            pltpu.VMEM((owned // 2, 256), F32),
             pltpu.VMEM((2, 16, nfaces), jnp.int16),
             pltpu.VMEM((2, 16, nfaces), BF16),
             pltpu.VMEM((owned, owned), BF16),
@@ -464,7 +453,7 @@
             pltpu.VMEM((rows, owned), F32),
             pltpu.VMEM((2, 2 * rows, owned), BF16),
             pltpu.VMEM((2, 96, owned), F8),
-            pltpu.VMEM((turns, n, count // 2, 128), F32),
+            pltpu.VMEM((turns, n, count // 4, 128), F32),
             pltpu.VMEM((turns - 1, 2, rows, halo), F32),
             pltpu.VMEM((turns - 1, 2, rows, halo), F32),
             pltpu.SemaphoreType.DMA((3,)),

time: 42.7 us -> 42.3 us (level)
  Pallas kernels: 41.9 us -> 41.4 us
    pallas_call x1, Pallas kernels: 41.1 us -> 40.7 us  [local(): pl.pallas_call(functools.partial(kernel, n), out_shape=(pltpu.VMEM((rows,...]
where the time goes in v6:
time: 42.3 us; the launch traced here: 42.1 us
  Pallas kernels  41.4 us (98%)
  between operations  0.64 us (2%)
    pallas_call x1, Pallas kernels, local(): pl.pallas_call(functools.partial(kernel, n), out_shape=(pltpu.VMEM((rows,...  40.7 us

profile of v6, /device:TPU:0, one launch (start us, length us, event | category | flops | bytes accessed | tf_op | source)
XLA Modules:
  0.0 42.1 jit_solution(17000501581249013967)
XLA Ops:
  0.6 40.7 %shard_map.104 = (f32[80,1024]{1,0:T(8,128)S(1)}, f32[16,20]{1,0:T(8,128)S(1)}) custom-call(f32[5,16,1024]{2,1,0:T(8,128)} %bitcast.12, bf16[5,5,16,1024]{3,2,1,0:T(8,128)(2,1)} %bitcast.10, f32[5,5,2,16]{3,2,1,0:T(2,128)} %bitcast.13, f32[5,20,1024]{2,1,0:T(8,128)} %bitcast.11, f32[1,20]{1,0:T(1,128)} %bitcast.16, s32[2,3072]{1,0:T(2,128)} %faces_ref.1, ...), custom_call_target="tpu_custom_call" | custom-call | tf_op jit(solution)/shard_map/pallas_call | solution.py:423
  41.3 0.7 %shard_map.105 = (f32[80,1024]{1,0:T(8,128)}, f32[16,20]{1,0:T(8,128)}) custom-call(f32[80,1024]{1,0:T(8,128)S(1)} %get-tuple-element.6.out_ref, f32[16,20]{1,0:T(8,128)S(1)} %get-tuple-element.7.part_ref), custom_call_target="tpu_custom_call" | custom-call | tf_op jit(solution)/shard_map/pallas_call | solution.py:479

commit v7 on v6

--- a/solution.py
+++ b/solution.py
@@ -278,7 +278,6 @@
 
     def wait_modal(turn):
         every = q_all.at[turn, pl.ds(0, n - 1)]
-        pltpu.make_async_copy(every, every, q_send.at[turn]).wait()
         pltpu.make_async_copy(every, every, q_recv.at[turn]).wait()
 
     def ghost_copies(turn):
@@ -337,7 +336,7 @@
                 build_ghost_matrix()
 
             for copy in ghost_copies(sweep - 1):
-                copy.wait()
+                copy.wait_recv()
             wait_modal(sweep - 1)
             low_part = ghost_in[sweep - 1, 0]
             up_part = ghost_in[sweep - 1, 1]
@@ -362,14 +361,24 @@
                 base = seed_ref[v] - term[spot]
                 base_ref[spot, :] = base
                 z_ref[spot, :] = base - z_ref[spot, :]
-
-        update(0)
+            update(0)
+
+        @pl.when(sweep == 0)
+        def _():
+            update(0)
+
         coupling()
         z_ref[...] = base_ref[...] - z_ref[...]
         update(1)
         start_exchange(sweep)
 
     out_hbm[...] = x_ref[...]
+    for turn in range(ITERS):
+        every = q_all.at[turn, pl.ds(0, n - 1)]
+        pltpu.make_async_copy(every, every, q_send.at[turn]).wait()
+        if turn < ITERS - 1:
+            for copy in ghost_copies(turn):
+                copy.wait_send()
     wait_modal(ITERS - 1)
     part_ref[...] = modal_sum(ITERS - 1)[:, :modes]
 

time: 42.3 us -> 42.3 us (level)
  no operation moved by 1% of the time
where the time goes in v7:
time: 42.3 us; the launch traced here: 42.1 us
  Pallas kernels  41.4 us (98%)
  between operations  0.64 us (2%)
    pallas_call x1, Pallas kernels, local(): pl.pallas_call(functools.partial(kernel, n), out_shape=(pltpu.VMEM((rows,...  40.7 us

profile of v7, /device:TPU:0, one launch (start us, length us, event | category | flops | bytes accessed | tf_op | source)
XLA Modules:
  0.0 42.1 jit_solution(3176019942126554001)
XLA Ops:
  0.6 40.7 %shard_map.104 = (f32[80,1024]{1,0:T(8,128)S(1)}, f32[16,20]{1,0:T(8,128)S(1)}) custom-call(f32[5,16,1024]{2,1,0:T(8,128)} %bitcast.12, bf16[5,5,16,1024]{3,2,1,0:T(8,128)(2,1)} %bitcast.10, f32[5,5,2,16]{3,2,1,0:T(2,128)} %bitcast.13, f32[5,20,1024]{2,1,0:T(8,128)} %bitcast.11, f32[1,20]{1,0:T(1,128)} %bitcast.16, s32[2,3072]{1,0:T(2,128)} %faces_ref.1, ...), custom_call_target="tpu_custom_call" | custom-call | tf_op jit(solution)/shard_map/pallas_call | solution.py:432
  41.3 0.7 %shard_map.105 = (f32[80,1024]{1,0:T(8,128)}, f32[16,20]{1,0:T(8,128)}) custom-call(f32[80,1024]{1,0:T(8,128)S(1)} %get-tuple-element.6.out_ref, f32[16,20]{1,0:T(8,128)S(1)} %get-tuple-element.7.part_ref), custom_call_target="tpu_custom_call" | custom-call | tf_op jit(solution)/shard_map/pallas_call | solution.py:488

commit v8 on v7

--- a/solution.py
+++ b/solution.py
@@ -27,11 +27,18 @@
 def bf16_factors(value):
     best_q = jnp.ones_like(value)
     best = jnp.abs(value - value.astype(BF16).astype(F32))
-    for k in range(1, CANDIDATES):
-        q = 1.0 + k / 128.0
-        miss = jnp.abs(value - (value * (1.0 / q)).astype(BF16).astype(F32) * q)
-        best_q = jnp.where(miss < best, q, best_q)
-        best = jnp.minimum(miss, best)
+
+    def group(turn, state):
+        best, best_q = state
+        first = turn.astype(F32) * (8.0 / 128.0) + 1.0
+        for k in range(8):
+            q = first + k / 128.0
+            miss = jnp.abs(value - (value / q).astype(BF16).astype(F32) * q)
+            best_q = jnp.where(miss < best, q, best_q)
+            best = jnp.minimum(miss, best)
+        return best, best_q
+
+    best, best_q = lax.fori_loop(0, CANDIDATES // 8, group, (best, best_q))
     return (value / best_q).astype(BF16), best_q.astype(BF16)
 
 

time: 42.3 us -> 42.3 us (level)
  no operation moved by 1% of the time
where the time goes in v8:
time: 42.3 us; the launch traced here: 42.1 us
  Pallas kernels  41.4 us (98%)
  between operations  0.64 us (2%)
    pallas_call x1, Pallas kernels, local(): pl.pallas_call(functools.partial(kernel, n), out_shape=(pltpu.VMEM((rows,...  40.7 us

profile of v8, /device:TPU:0, one launch (start us, length us, event | category | flops | bytes accessed | tf_op | source)
XLA Modules:
  0.0 42.1 jit_solution(7251382089483640766)
XLA Ops:
  0.6 40.7 %shard_map.104 = (f32[80,1024]{1,0:T(8,128)S(1)}, f32[16,20]{1,0:T(8,128)S(1)}) custom-call(f32[5,16,1024]{2,1,0:T(8,128)} %bitcast.12, bf16[5,5,16,1024]{3,2,1,0:T(8,128)(2,1)} %bitcast.10, f32[5,5,2,16]{3,2,1,0:T(2,128)} %bitcast.13, f32[5,20,1024]{2,1,0:T(8,128)} %bitcast.11, f32[1,20]{1,0:T(1,128)} %bitcast.16, s32[2,3072]{1,0:T(2,128)} %faces_ref.1, ...), custom_call_target="tpu_custom_call" | custom-call | tf_op jit(solution)/shard_map/pallas_call | solution.py:439
  41.3 0.7 %shard_map.105 = (f32[80,1024]{1,0:T(8,128)}, f32[16,20]{1,0:T(8,128)}) custom-call(f32[80,1024]{1,0:T(8,128)S(1)} %get-tuple-element.6.out_ref, f32[16,20]{1,0:T(8,128)S(1)} %get-tuple-element.7.part_ref), custom_call_target="tpu_custom_call" | custom-call | tf_op jit(solution)/shard_map/pallas_call | solution.py:495
